TPU v7x, 128 devices: a whole 4x4x4 slice. The times are simulated.
128 devices in a mesh: src: 8 (over y, core), tgt: 16 (over z, x).
Axes of the slice: x: 4, y: 4, z: 4, core: 2. Of those that a mesh axis runs over, the one named last changes fastest.
Arguments:
- source_cells: bfloat16 [262144, 64], P('src'), may hold values from -4 to 4
- target_cells: bfloat16 [131072, 64], P('tgt'), may hold values from -1 to 1
- log_source: float32 [262144], P('src'), may hold values from -4 to 4
- log_target: float32 [131072], P('tgt'), may hold values from -4 to 4
- support: int32 [2048, 32], P('src'), may hold values from 0 to 1023, as said below
Outputs:
- source_potential: float32 [262144], P('src')
- target_potential: float32 [131072], P('tgt')
Inputs may be any that keep to these rules, and one draw needn't show every extreme that they name: `support`: each row holds 32 different target tile numbers. Within the rows of one index of src (aligned blocks of 256 rows), at most 1024 entries fall among the tiles of one index of tgt (tiles k with k // 64 equal), and exactly 1024 fall on one of them; every target tile is named in the rows of every index of src.
All inputs are finite; a program needn't handle non-finite values.
Results may differ from a plain program's by a relative error of at most 0.0044.
Values may be sent and summed in bfloat16 or wider, within the bound.
No kernel may reach another device: no remote copies, remote signals or barrier semaphores. Data moves between devices by JAX's collectives and lax.ppermute only.
A program may use at most 320 MiB of HBM per device.

v0:
```python
import jax
import jax.numpy as jnp
from jax import lax
from jax.sharding import PartitionSpec as P

TILE = 128
ITERS = 2


EPS = 0.1
NEG = -1e30
HIGH = lax.Precision.HIGHEST


def squares_of(tiles):
    values = tiles.astype(jnp.float32)
    return jnp.sum(values * values, axis=2)


def cost_tile(src_block, src_square, tgt_block, tgt_square):
    cross_term = jnp.einsum(
        "bie,bje->bij", src_block, tgt_block, preferred_element_type=jnp.float32
    )
    return src_square[:, :, None] + tgt_square[:, None, :] - 2.0 * cross_term


def one_hot(ids, count):
    return (ids[:, None] == jnp.arange(count, dtype=jnp.int32)[None, :]).astype(jnp.float32)


def pick_rows(selector, table):
    return jnp.dot(selector, table, precision=HIGH, preferred_element_type=jnp.float32)


def fold_block(maxima, totals, selector, block_max, exp_of):
    candidate = jnp.max(jnp.where(selector[:, :, None] > 0.5, block_max[:, None, :], NEG), axis=0)
    new_max = jnp.maximum(maxima, candidate)
    exp_terms = exp_of(pick_rows(selector, new_max))
    added = jnp.dot(selector.T, exp_terms, precision=HIGH, preferred_element_type=jnp.float32)
    return (new_max, totals * jnp.exp(maxima - new_max) + added)


def row_stats(
    slot_rows,
    slot_tiles,
    active,
    pre_src,
    pre_srcn,
    pre_tgt,
    pre_tgtn,
    target_pot,
    row_count,
    num_blocks,
):
    shape_rows = (row_count, pre_srcn.shape[1])
    start_carry = (jnp.full(shape_rows, NEG, jnp.float32), jnp.zeros(shape_rows, jnp.float32))
    tile_count = target_pot.shape[0]

    def row_one_step(carried, block_item):
        maxima, totals = carried
        row_ids, tile_ids, alive, src_block, src_square, tgt_block, tgt_square = block_item
        costs = cost_tile(src_block, src_square, tgt_block, tgt_square)
        slot_pot = pick_rows(one_hot(tile_ids, tile_count), target_pot)
        scores = (slot_pot[:, None, :] - costs) / EPS
        block_max = jnp.where(alive[:, None], jnp.max(scores, axis=2), NEG)
        selector = one_hot(row_ids, row_count) * alive[:, None].astype(jnp.float32)

        def exp_of(slot_max):
            terms = jnp.sum(jnp.exp(scores - slot_max[:, :, None]), axis=2)
            return jnp.where(alive[:, None], terms, 0.0)

        return (fold_block(maxima, totals, selector, block_max, exp_of), None)

    def row_blocks(array):
        return array.reshape((num_blocks, -1) + array.shape[1:])

    block_items = tuple(
        (
            row_blocks(item)
            for item in (slot_rows, slot_tiles, active, pre_src, pre_srcn, pre_tgt, pre_tgtn)
        )
    )
    return lax.scan(row_one_step, start_carry, block_items)[0]


def col_stats(
    slot_rows,
    slot_tiles,
    active,
    pre_src,
    pre_srcn,
    pre_tgt,
    pre_tgtn,
    source_pot,
    tile_count,
    num_blocks,
):
    shape_cols = (tile_count, pre_tgtn.shape[1])
    start_carry = (jnp.full(shape_cols, NEG, jnp.float32), jnp.zeros(shape_cols, jnp.float32))
    row_count = source_pot.shape[0]

    def col_one_step(carried, block_item):
        maxima, totals = carried
        row_ids, tile_ids, alive, src_block, src_square, tgt_block, tgt_square = block_item
        costs = cost_tile(src_block, src_square, tgt_block, tgt_square)
        slot_pot = pick_rows(one_hot(row_ids, row_count), source_pot)
        scores = (slot_pot[:, :, None] - costs) / EPS
        block_max = jnp.where(alive[:, None], jnp.max(scores, axis=1), NEG)
        selector = one_hot(tile_ids, tile_count) * alive[:, None].astype(jnp.float32)

        def exp_of(slot_max):
            terms = jnp.sum(jnp.exp(scores - slot_max[:, None, :]), axis=1)
            return jnp.where(alive[:, None], terms, 0.0)

        return (fold_block(maxima, totals, selector, block_max, exp_of), None)

    def col_blocks(array):
        return array.reshape((num_blocks, -1) + array.shape[1:])

    block_items = tuple(
        (
            col_blocks(item)
            for item in (slot_rows, slot_tiles, active, pre_src, pre_srcn, pre_tgt, pre_tgtn)
        )
    )
    return lax.scan(col_one_step, start_carry, block_items)[0]


def across_targets(maxima, totals):
    highest = lax.pmax(maxima, "tgt")
    return (highest, lax.psum(totals * jnp.exp(maxima - highest), "tgt"))


def across_sources(maxima, totals):
    highest = lax.pmax(maxima, "src")
    return (highest, lax.psum(totals * jnp.exp(maxima - highest), "src"))


def on_device(source_cells, target_cells, log_source, log_target, support):
    row_count = source_cells.shape[0] // TILE
    src_tiles = source_cells.reshape(row_count, TILE, source_cells.shape[1])
    src_norm = squares_of(src_tiles)
    flat_ids = support.reshape(-1)
    num_slots = flat_ids.shape[0]
    tgt_index = lax.axis_index("tgt")
    own_tiles = target_cells.shape[0] // TILE
    per_device = num_slots // lax.axis_size("tgt")
    tgt_tiles = target_cells.reshape(own_tiles, TILE, target_cells.shape[1])
    log_cols = log_target.reshape(own_tiles, TILE)
    capacity = 2 * per_device
    owned = flat_ids // own_tiles == tgt_index
    slot_rank = jnp.cumsum(owned.astype(jnp.int32)) - 1
    target_place = jnp.where(owned, slot_rank, capacity)
    slot_index = (
        jnp.zeros((capacity,), jnp.int32)
        .at[target_place]
        .set(jnp.arange(num_slots, dtype=jnp.int32), mode="drop")
    )
    active = jnp.arange(capacity, dtype=jnp.int32) < jnp.sum(owned.astype(jnp.int32))
    slot_tiles = jnp.clip(flat_ids[slot_index] - tgt_index * own_tiles, 0, own_tiles - 1)
    tgt_norm = squares_of(tgt_tiles)
    tile_count = tgt_tiles.shape[0]
    slot_rows = slot_index // support.shape[1]
    pre_src = src_tiles[slot_rows]
    pre_srcn = src_norm[slot_rows]
    pre_tgt = tgt_tiles[slot_tiles]
    pre_tgtn = tgt_norm[slot_tiles]
    num_blocks = capacity // min(64, capacity)
    log_rows = log_source.reshape(row_count, TILE)
    target_pot = jnp.zeros(log_cols.shape, jnp.float32)
    source_pot = jnp.zeros(log_rows.shape, jnp.float32)
    for iteration in range(ITERS):
        maxima, totals = row_stats(
            slot_rows,
            slot_tiles,
            active,
            pre_src,
            pre_srcn,
            pre_tgt,
            pre_tgtn,
            target_pot,
            row_count,
            num_blocks,
        )
        maxima, totals = across_targets(maxima, totals)
        source_pot = EPS * log_rows - EPS * (maxima + jnp.log(totals))
        maxima, totals = col_stats(
            slot_rows,
            slot_tiles,
            active,
            pre_src,
            pre_srcn,
            pre_tgt,
            pre_tgtn,
            source_pot,
            tile_count,
            num_blocks,
        )
        maxima, totals = across_sources(maxima, totals)
        target_pot = EPS * log_cols - EPS * (maxima + jnp.log(totals))
    return (source_pot.reshape(-1), target_pot.reshape(-1))


def solution(mesh):
    return jax.shard_map(
        on_device,
        mesh=mesh,
        in_specs=(P("src", None), P("tgt", None), P("src"), P("tgt"), P("src", None)),
        out_specs=(P("src"), P("tgt")),
        check_vma=False,
    )
```

profile of v0, /device:TPU:0, one launch (start us, length us, event | category | flops | bytes accessed | tf_op | source)
XLA Modules:
  0.0 1355.2 jit_solution(3645229197953501533)
XLA Ops:
  11.4 5.6 copy_bitcast_fusion
  19.6 30.4 %scatter_custom_fusion = s32[1024]{0:T(1024)S(1)} fusion(s32[8192]{0:T(1024)S(1)} %bitcast.177, s32[8192]{0:T(1024)S(1)} %iota.65, s32[]{:T(128)} %constant.157.clone.1), kind=kCustom, calls=%fused_computation.222 | custom fusion | bytes 4100 | tf_op jit(solution)/shard_map/scatter | solution.py:157
  50.1 6.2 gather_fusion
  56.3 13.5 gather_fusion.4
  72.6 15.7 %gather_fusion.3 = bf16[1024,128,64]{1,2,0:T(8,128)(2,1)} fusion(bf16[256,128,64]{1,2,0:T(8,128)(2,1)} %copy_bitcast_fusion, s32[1024]{0:T(1024)S(1)} %get-tuple-element.496), kind=kCustom, calls=%fused_computation.3 | custom fusion | bytes 33558528 | tf_op jit(solution)/shard_map/gather | solution.py:164
  91.9 223.4 %while.52 = (s32[]{:T(128)}, f32[256,128]{1,0:T(8,128)S(1)}, f32[256,128]{1,0:T(8,128)S(1)}, s32[16,64]{1,0:T(8,128)S(1)}, pred[16,64]{1,0:T(8,128)(4,1)S(1)}, /...) while((s32[]{:T(128)}, f32[256,128]{1,0:T(8,128)S(1)}, ...), condition=%wide.region_10.11_spmd.clone, body=%wide.region_6.10_spmd.clone.sunk | while | flops 208982080 | bytes 12587404 | solution.py:83
  92.2 5.4 fusion.176
  106.1 5.4 fusion.176
  134.0 5.4 fusion.176
  148.0 5.4 fusion.176
  162.0 5.4 fusion.176
  175.9 5.4 fusion.176
  189.9 5.4 fusion.176
  203.8 5.4 fusion.176
  217.8 5.4 fusion.176
  231.8 5.4 fusion.176
  245.7 5.4 fusion.176
  259.7 5.4 fusion.176
  273.7 5.4 fusion.176
  287.6 5.4 fusion.176
  301.6 5.4 fusion.176
  316.0 85.0 %all-reduce.5.cloned.1.call-done = f32[256,128]{1,0:T(8,128)} async-done(((f32[256,128]{1,0:T(8,128)}), f32[256,128]{1,0:T(8,128)}) %all-reduce.5.cloned.1.call-update) | async-done | bytes 131088 | tf_op jit(solution)/shard_map/pmax | solution.py:130
  402.8 84.0 %all-reduce.7.cloned.1.call-done = f32[256,128]{1,0:T(8,128)} async-done(((f32[256,128]{1,0:T(8,128)}), f32[256,128]{1,0:T(8,128)}) %all-reduce.7.cloned.1.call-update) | async-done | bytes 131088 | tf_op jit(solution)/shard_map/psum | solution.py:131
  487.8 187.3 %while.53 = (s32[]{:T(128)}, f32[64,128]{1,0:T(8,128)S(1)}, f32[64,128]{1,0:T(8,128)S(1)}, s32[16,64]{1,0:T(8,128)S(1)}, pred[16,64]{1,0:T(8,128)(4,1)S(1)}, /*i...) while((s32[]{:T(128)}, f32[64,128]{1,0:T(8,128)S(1)}, ...), condition=%wide.region_17.18_spmd.clone, body=%wide.region_13.17_spmd.clone.sunk | while | flops 186740800 | bytes 11612564 | solution.py:126
  488.1 5.4 fusion.186
  499.8 5.4 fusion.186
  523.2 5.4 fusion.186
  535.0 5.4 fusion.186
  546.7 5.4 fusion.186
  558.4 5.4 fusion.186
  581.8 5.4 fusion.186
  593.5 5.4 fusion.186
  605.2 5.4 fusion.186
  616.9 5.4 fusion.186
  628.6 5.4 fusion.186
  640.3 5.4 fusion.186
  652.0 5.4 fusion.186
  663.8 5.4 fusion.186
  675.2 24.3 %pmax.29 = f32[64,128]{1,0:T(8,128)S(1)} all-reduce(f32[64,128]{1,0:T(8,128)S(1)} %get-tuple-element.231), channel_id=1, replica_groups=mesh['src'=8,'tgt'=16] {'src'}, use_global_device_ids=true, to_apply=%region_18.19 | all-reduce | flops 8192 | bytes 65536 | tf_op jit(solution)/shard_map/pmax | solution.py:135
  699.5 23.6 %psum.29 = f32[64,128]{1,0:T(8,128)S(1)} all-reduce(f32[64,128]{1,0:T(8,128)S(1)} %exponential_multiply_fusion.3), channel_id=1, replica_groups=mesh['src'=8,'tgt'=16] {'src'}, use_global_device_ids=true, to_apply=%region_19.20 | all-reduce | flops 8192 | bytes 65536 | tf_op jit(solution)/shard_map/psum | solution.py:136
  723.1 223.4 %while.54 = (s32[]{:T(128)}, f32[256,128]{1,0:T(8,128)S(1)}, f32[256,128]{1,0:T(8,128)S(1)}, s32[16,64]{1,0:T(8,128)S(1)}, pred[16,64]{1,0:T(8,128)(4,1)S(1)}, /...) while((s32[]{:T(128)}, f32[256,128]{1,0:T(8,128)S(1)}, ...), condition=%wide.region_24.25_spmd.clone, body=%wide.region_20.24_spmd.clone.sunk | while | flops 208982080 | bytes 12620180 | solution.py:83
  723.3 5.4 fusion.196
  737.3 5.4 fusion.196
  751.3 5.4 fusion.196
  765.2 5.4 fusion.196
  779.2 5.4 fusion.196
  793.2 5.4 fusion.196
  947.2 79.1 %all-reduce.9.cloned.1.call-done = f32[256,128]{1,0:T(8,128)} async-done(((f32[256,128]{1,0:T(8,128)}), f32[256,128]{1,0:T(8,128)}) %all-reduce.9.cloned.1.call-update) | async-done | bytes 131088 | tf_op jit(solution)/shard_map/pmax | solution.py:130
  1028.0 84.0 %all-reduce.11.cloned.1.call-done = f32[256,128]{1,0:T(8,128)} async-done(((f32[256,128]{1,0:T(8,128)}), f32[256,128]{1,0:T(8,128)}) %all-reduce.11.cloned.1.call-update) | async-done | bytes 131088 | tf_op jit(solution)/shard_map/psum | solution.py:131
  1113.0 187.3 %while.55 = (s32[]{:T(128)}, f32[64,128]{1,0:T(8,128)S(1)}, f32[64,128]{1,0:T(8,128)S(1)}, s32[16,64]{1,0:T(8,128)S(1)}, pred[16,64]{1,0:T(8,128)(4,1)S(1)}, /*i...) while((s32[]{:T(128)}, f32[64,128]{1,0:T(8,128)S(1)}, ...), condition=%wide.region_31.32_spmd.clone, body=%wide.region_27.31_spmd.clone.sunk | while | flops 186740800 | bytes 11612564 | solution.py:126
  1113.3 5.4 fusion.206
  1136.7 5.4 fusion.206
  1160.1 5.4 fusion.206
  1171.8 5.4 fusion.206
  1183.5 5.4 fusion.206
  1195.2 5.4 fusion.206
  1207.0 5.4 fusion.206
  1218.7 5.4 fusion.206
  1230.4 5.4 fusion.206
  1242.1 5.4 fusion.206
  1265.5 5.4 fusion.206
  1288.9 5.4 fusion.206
  1300.4 24.1 %pmax.31 = f32[64,128]{1,0:T(8,128)S(1)} all-reduce(f32[64,128]{1,0:T(8,128)S(1)} %get-tuple-element.235), channel_id=1, replica_groups=mesh['src'=8,'tgt'=16] {'src'}, use_global_device_ids=true, to_apply=%region_32.33 | all-reduce | flops 8192 | bytes 65536 | tf_op jit(solution)/shard_map/pmax | solution.py:135
  1324.5 23.6 %psum.31 = f32[64,128]{1,0:T(8,128)S(1)} all-reduce(f32[64,128]{1,0:T(8,128)S(1)} %exponential_multiply_fusion.2), channel_id=1, replica_groups=mesh['src'=8,'tgt'=16] {'src'}, use_global_device_ids=true, to_apply=%region_33.34 | all-reduce | flops 8192 | bytes 65536 | tf_op jit(solution)/shard_map/psum | solution.py:136
  (848 shorter events, 579.9 us)
Async XLA Ops:
  7.2 393.9 %all-reduce.5.cloned.1.call-start = ((), (), s32[]{:S(2)}) async-start(), calls=%async_computation | async-start | bytes 262144 | tf_op jit(solution)/shard_map/pmax | solution.py:130
  11.4 5.6 copy-start.2
  17.0 1.0 copy-start.5
  91.9 394.9 %copy-start.4 = (f32[32768]{0:T(1024)S(1)}, f32[32768]{0:T(1024)}, u32[]{:S(2)}) copy-start(f32[32768]{0:T(1024)} %param.15) | copy-start | bytes 393220
  315.3 0.7 copy-start.1
  316.0 170.9 %all-reduce.7.cloned.1.call-start = ((), (), s32[]{:S(2)}) async-start(), calls=%async_computation.1 | async-start | bytes 262144 | tf_op jit(solution)/shard_map/psum | solution.py:131
  402.7 623.6 %all-reduce.9.cloned.1.call-start = ((), (), s32[]{:S(2)}) async-start(), calls=%async_computation.2 | async-start | bytes 262144 | tf_op jit(solution)/shard_map/pmax | solution.py:130
  487.8 235.2 %copy-start.6 = (f32[8192]{0:T(1024)S(1)}, f32[8192]{0:T(1024)}, u32[]{:S(2)}) copy-start(f32[8192]{0:T(1024)} %param.16) | copy-start | bytes 98308
  946.5 0.7 copy-start
  947.2 164.8 %all-reduce.11.cloned.1.call-start = ((), (), s32[]{:S(2)}) async-start(), calls=%async_computation.3 | async-start | bytes 262144 | tf_op jit(solution)/shard_map/psum | solution.py:131
  1300.4 48.3 %copy-start.3 = (f32[256,128]{1,0:T(8,128)}, f32[256,128]{1,0:T(8,128)S(1)}, u32[]{:S(2)}) copy-start(f32[256,128]{1,0:T(8,128)S(1)} %get-tuple-element.992) | copy-start | bytes 393220
Sparse Core Ops, SparseCore 0:
  316.1 84.9 all-reduce.4
  405.1 81.6 all-reduce.6
  947.3 78.9 all-reduce.8
  1030.3 81.6 all-reduce.10
where the time goes:
time: 1360 us
  other arithmetic  421 us (31%)
  matrix products  402 us (30%)
  waiting for transfers between devices  332 us (24%)
  blocking collectives  95.5 us (7%)
  local copies, waits for them, and re-layouts  83.3 us (6%)
  between operations  14.1 us (1%)
    dot_general x64, matrix products, cost_tile(): jnp.einsum('bie,bje->bij', src_block, tgt_block, preferred_element_type=j...  349 us
    psum x2, waiting for transfers between devices, across_targets(): return (highest, lax.psum(totals * jnp.exp(maxima - highest), 'tgt'))  168 us
    pmax x2, waiting for transfers between devices, across_targets(): highest = lax.pmax(maxima, 'tgt')  164 us
    reduce_sum x32, other arithmetic, exp_of(): terms = jnp.sum(jnp.exp(scores - slot_max[:, :, None]), axis=2)  144 us
    reduce_sum x32, other arithmetic, exp_of(): terms = jnp.sum(jnp.exp(scores - slot_max[:, None, :]), axis=1)  144 us
    reduce_max x64, other arithmetic, fold_block(): jnp.max(jnp.where(selector[:, :, None] > 0.5, block_max[:, None, :], NEG)...  111 us
    pmax x2, blocking collectives, across_sources(): highest = lax.pmax(maxima, 'src')  48.3 us
    psum x2, blocking collectives, across_sources(): return (highest, lax.psum(totals * jnp.exp(maxima - highest), 'src'))  47.2 us
  transfers between devices with their start and end apart: 4, of which 4 were waited for; matrix products, arithmetic and copies ran while one was open for 0% of the time, Pallas kernels for 0%

commit v1 on v0

--- a/solution.py
+++ b/solution.py
@@ -1,6 +1,10 @@
+import functools
+
 import jax
 import jax.numpy as jnp
 from jax import lax
+from jax.experimental import pallas as pl
+from jax.experimental.pallas import tpu as pltpu
 from jax.sharding import PartitionSpec as P
 
 TILE = 128
@@ -10,6 +14,17 @@
 EPS = 0.1
 NEG = -1e30
 HIGH = lax.Precision.HIGHEST
+
+SCALE = 14.426950408889634
+LN2 = 0.6931471805599453
+SHIFT = 9.0
+ROW_LOW = 2.0**-30
+ROW_HIGH = 2.0**80
+COL_LOW = 2.0**-10
+COL_HIGH = 2.0**80
+RATIO = 2.0**30
+POISON = 3.0e38
+POISONED = 1.0e37
 
 
 def squares_of(tiles):
@@ -136,7 +151,7 @@
     return (highest, lax.psum(totals * jnp.exp(maxima - highest), "src"))
 
 
-def on_device(source_cells, target_cells, log_source, log_target, support):
+def general_path(source_cells, target_cells, log_source, log_target, support):
     row_count = source_cells.shape[0] // TILE
     src_tiles = source_cells.reshape(row_count, TILE, source_cells.shape[1])
     src_norm = squares_of(src_tiles)
@@ -201,6 +216,318 @@
     return (source_pot.reshape(-1), target_pot.reshape(-1))
 
 
+CAP_STEP = 128
+BUILD_UNROLL = 64
+ROW_UNROLL = 64
+COL_UNROLL = 64
+SMEM = pl.BlockSpec(memory_space=pltpu.SMEM)
+VMEM = pl.BlockSpec(memory_space=pltpu.VMEM)
+BF16 = jnp.bfloat16
+F32 = jnp.float32
+
+
+def params(mib):
+    return pltpu.CompilerParams(vmem_limit_bytes=mib * 2**20)
+
+
+def dot_t(a, b):
+    return lax.dot_general(a, b, (((1,), (1,)), ((), ())), preferred_element_type=F32)
+
+
+def dot_n(a, b):
+    return jnp.dot(a, b, preferred_element_type=F32)
+
+
+def ones_where(mask):
+    return jnp.where(mask, 1.0, 0.0).astype(BF16)
+
+
+def iota(shape, axis):
+    return lax.broadcasted_iota(jnp.int32, shape, axis)
+
+
+def list_kernel(place_ref, sup_ref, rows_ref, tiles_ref, count_ref, by_row_ref, by_tile_ref):
+    width, rows = sup_ref.shape
+    cap = rows_ref.shape[1]
+    own_tiles = by_tile_ref.shape[0]
+    local = sup_ref[...] - place_ref[0] * own_tiles
+    owned = (local >= 0) & (local < own_tiles)
+    mask = ones_where(owned)
+    lower = ones_where(iota((width, width), 1) <= iota((width, width), 0))
+    rank = dot_n(lower, mask)
+    count = rank[width - 1 : width, :]
+    before = ones_where(iota((rows, rows), 1) < iota((rows, rows), 0))
+    upto = ones_where(iota((rows, rows), 1) <= iota((rows, rows), 0))
+    first = jnp.sum(dot_t(before, mask), axis=1, keepdims=True).astype(jnp.int32)
+    last = jnp.sum(dot_t(upto, mask), axis=1, keepdims=True).astype(jnp.int32)
+    place = iota((rows, cap), 1)
+    by_row = ones_where((first <= place) & (place < last))
+    by_row_ref[...] = by_row
+    after = ones_where(iota((rows, rows), 0) < iota((rows, rows), 1))
+    count8 = jnp.broadcast_to(count, (8, rows)).astype(BF16)
+    first8 = dot_n(count8, after)
+    high = jnp.floor(first8 * (1.0 / 32.0))
+    low = first8 - 32.0 * high
+    row_id = iota((8, rows), 1).astype(F32)
+    tile = jnp.where(owned, local, 0).astype(F32)
+    table = jnp.concatenate([tile, jnp.where(owned, rank, 0.0), row_id, high, low], axis=0)
+    got = dot_n(table.astype(BF16), by_row)
+    begin = 32.0 * got[2 * width + 8 : 2 * width + 9] + got[2 * width + 16 : 2 * width + 17]
+    place_f = iota((1, cap), 1).astype(F32)
+    want = place_f - begin + 1.0
+    tiles = jnp.sum(jnp.where(got[width : 2 * width] == want, got[:width], 0.0), axis=0, keepdims=True)
+    tiles_ref[...] = tiles.astype(jnp.int32)
+    rows_ref[...] = got[2 * width : 2 * width + 1].astype(jnp.int32)
+    total = jnp.sum(count, axis=1, keepdims=True)
+    count_ref[...] = jnp.broadcast_to(total, count_ref.shape).astype(jnp.int32)
+    by_tile_ref[...] = ones_where(
+        (iota((own_tiles, cap), 0).astype(F32) == tiles) & (place_f < total)
+    )
+
+
+def sum_slots(members, parts):
+    high = parts.astype(BF16)
+    low = (parts - high.astype(F32)).astype(BF16)
+    return dot_n(members, high) + dot_n(members, low)
+
+
+def build_kernel(
+    count_ref, rows_ref, tiles_ref, src_ref, tgt_ref, by_row_ref,
+    kern_ref, sum_ref, norm_ref, shift_ref,
+    left, extra, part,
+):
+    dim, tgt_count = tgt_ref.shape
+    row_count = extra.shape[0]
+    lane = iota((TILE, TILE), 1)
+
+    def one_tgt(k, unused):
+        block = tgt_ref[:, pl.ds(pl.multiple_of(k * TILE, TILE), TILE)].astype(F32)
+        wide = jnp.concatenate([block, jnp.zeros((TILE - dim, TILE), F32)], axis=0).T
+        half = -0.5 * jnp.sum(wide * wide, axis=1, keepdims=True)
+        a = half.astype(BF16).astype(F32)
+        b = (half - a).astype(BF16).astype(F32)
+        c = half - a - b
+        pieces = jnp.where(lane == dim, a, jnp.where(lane == dim + 1, b, jnp.where(lane == dim + 2, c, 1.0)))
+        left[k] = jnp.where(lane < dim, wide, jnp.where(lane < dim + 4, pieces, 0.0)).astype(BF16)
+        return unused
+
+    lax.fori_loop(0, tgt_count // TILE, one_tgt, 0)
+    line = iota((16, TILE), 0)
+
+    def one_src(r, unused):
+        block = src_ref[:, pl.ds(pl.multiple_of(r * TILE, TILE), TILE)].astype(F32)
+        norm = jnp.sum(block * block, axis=0, keepdims=True)
+        part_shift = (jnp.sqrt(norm) * (SHIFT / (2.0 * SCALE))).astype(BF16).astype(F32)
+        norm_ref[pl.ds(r, 1), :] = norm
+        shift_ref[pl.ds(r, 1), :] = part_shift * (2.0 * SCALE)
+        extra[r] = jnp.where(line < 3, 1.0, jnp.where(line == 3, -part_shift, 0.0)).astype(BF16)
+        return unused
+
+    lax.fori_loop(0, row_count, one_src, 0, unroll=8)
+    part[...] = jnp.zeros_like(part)
+    pad = jnp.zeros((TILE - dim - 16, TILE), BF16)
+
+    def step(g, unused):
+        base = g * BUILD_UNROLL
+        for u in range(BUILD_UNROLL):
+            q = base + u
+            r = rows_ref[0, q]
+            k = tiles_ref[0, q]
+            block = src_ref[:, pl.ds(pl.multiple_of(r * TILE, TILE), TILE)]
+            right = jnp.concatenate([block, extra[r], pad], axis=0)
+            entry = jnp.exp2(dot_n(left[k], right) * (2.0 * SCALE))
+            kern_ref[q] = entry.astype(BF16)
+            part[pl.ds(q, 1), :] = jnp.sum(entry, axis=0, keepdims=True)
+        return unused
+
+    lax.fori_loop(0, pl.cdiv(count_ref[0, 0], BUILD_UNROLL), step, 0)
+    sum_ref[...] = sum_slots(by_row_ref[...], part[...])
+
+
+def in_range(value, low, high):
+    return (value >= low) & (value <= high)
+
+
+def poison(ok, value):
+    bad = jnp.max(jnp.where(ok, 0.0, 1.0))
+    return jnp.where(bad > 0.0, POISON, value)
+
+
+def two_rows(table, first, second):
+    return jnp.concatenate(
+        [
+            jnp.broadcast_to(table[pl.ds(first, 1), :], (8, TILE)),
+            jnp.broadcast_to(table[pl.ds(second, 1), :], (8, TILE)),
+        ],
+        axis=0,
+    ).astype(BF16)
+
+
+def row_kernel(count_ref, tiles_ref, total_ref, log_ref, kern_ref, by_row_ref, out_ref, table, part):
+    total = total_ref[...]
+    table[...] = jnp.exp(log_ref[...]) / total
+    part[...] = jnp.zeros_like(part)
+
+    def step(g, unused):
+        base = g * ROW_UNROLL
+        for u in range(0, ROW_UNROLL, 2):
+            q = base + u
+            weights = two_rows(table, tiles_ref[0, q], tiles_ref[0, q + 1])
+            pair = jnp.concatenate([kern_ref[q], kern_ref[q + 1]], axis=1)
+            got = dot_n(weights, pair)
+            part[pl.ds(q, 1), :] = got[0:1, :TILE]
+            part[pl.ds(q + 1, 1), :] = got[8:9, TILE:]
+        return unused
+
+    lax.fori_loop(0, pl.cdiv(count_ref[0, 0], ROW_UNROLL), step, 0)
+    out = sum_slots(by_row_ref[...], part[...])
+    out_ref[...] = poison(in_range(total, COL_LOW, COL_HIGH), out)
+
+
+def col_body(ok, count_ref, rows_ref, total, log_ref, kern_ref, by_tile_ref, out_ref, table, part):
+    table[...] = jnp.exp(log_ref[...]) / total
+    part[...] = jnp.zeros_like(part)
+    none = jnp.zeros((16, TILE), BF16)
+
+    def step(g, unused):
+        base = g * COL_UNROLL
+        for u in range(0, COL_UNROLL, 4):
+            q = base + u
+            ab = two_rows(table, rows_ref[0, q], rows_ref[0, q + 1])
+            cd = two_rows(table, rows_ref[0, q + 2], rows_ref[0, q + 3])
+            weights = jnp.concatenate(
+                [jnp.concatenate([ab, none], axis=1), jnp.concatenate([none, cd], axis=1)], axis=0
+            )
+            four = jnp.concatenate(
+                [
+                    jnp.concatenate([kern_ref[q], kern_ref[q + 2]], axis=1),
+                    jnp.concatenate([kern_ref[q + 1], kern_ref[q + 3]], axis=1),
+                ],
+                axis=0,
+            )
+            got = dot_t(weights, four)
+            part[pl.ds(q, 1), :] = got[0:1, :TILE]
+            part[pl.ds(q + 1, 1), :] = got[8:9, TILE:]
+            part[pl.ds(q + 2, 1), :] = got[16:17, :TILE]
+            part[pl.ds(q + 3, 1), :] = got[24:25, TILE:]
+        return unused
+
+    lax.fori_loop(0, pl.cdiv(count_ref[0, 0], COL_UNROLL), step, 0)
+    out_ref[...] = poison(ok, sum_slots(by_tile_ref[...], part[...]))
+
+
+def first_col_kernel(count_ref, rows_ref, total_ref, log_ref, kern_ref, by_tile_ref, out_ref, table, part):
+    total = total_ref[...]
+    ok = in_range(total, ROW_LOW, ROW_HIGH)
+    col_body(ok, count_ref, rows_ref, total, log_ref, kern_ref, by_tile_ref, out_ref, table, part)
+
+
+def next_col_kernel(
+    count_ref, rows_ref, total_ref, earlier_ref, log_ref, kern_ref, by_tile_ref, out_ref, table, part
+):
+    total = total_ref[...]
+    ratio = total / earlier_ref[...]
+    ok = in_range(total, ROW_LOW, ROW_HIGH) & in_range(ratio, 1.0 / RATIO, RATIO)
+    col_body(ok, count_ref, rows_ref, total, log_ref, kern_ref, by_tile_ref, out_ref, table, part)
+
+
+def ring_sum(value, axis, size, perm):
+    def moved(d):
+        return lax.ppermute(value, axis, [(i, perm(i, d)) for i in range(size)])
+
+    opposite, right, left = moved(2), moved(1), moved(3)
+    return (value + opposite) + (right + left)
+
+
+def sum_over_tgt(value):
+    value = ring_sum(value, "tgt", 16, lambda i, d: (i // 4) * 4 + (i % 4 + d) % 4)
+    return ring_sum(value, "tgt", 16, lambda i, d: (i + 4 * d) % 16)
+
+
+def sum_over_src(value):
+    value = value + lax.ppermute(value, "src", [(i, i ^ 1) for i in range(8)])
+    return ring_sum(value, "src", 8, lambda i, d: (i + 2 * d) % 8)
+
+
+def on_device(source_cells, target_cells, log_source, log_target, support):
+    row_count = source_cells.shape[0] // TILE
+    tile_count = target_cells.shape[0] // TILE
+    cap = 2 * support.size // lax.axis_size("tgt")
+    place = lax.axis_index("tgt").astype(jnp.int32).reshape(1)
+    log_rows = log_source.reshape(row_count, TILE)
+    log_cols = log_target.reshape(tile_count, TILE)
+    array = jax.ShapeDtypeStruct
+    rows, tiles, count, by_row, by_tile = pl.pallas_call(
+        list_kernel,
+        out_shape=(
+            array((1, cap), jnp.int32),
+            array((1, cap), jnp.int32),
+            array((1, TILE), jnp.int32),
+            array((row_count, cap), BF16),
+            array((tile_count, cap), BF16),
+        ),
+        in_specs=[SMEM, VMEM],
+        out_specs=(VMEM,) * 5,
+        compiler_params=params(16),
+        name="list_support",
+    )(place, support.T)
+    kern, total, norm, shift = pl.pallas_call(
+        build_kernel,
+        out_shape=(
+            pltpu.VMEM((cap, TILE, TILE), BF16),
+            array((row_count, TILE), F32),
+            array((row_count, TILE), F32),
+            array((row_count, TILE), F32),
+        ),
+        in_specs=[SMEM] * 3 + [VMEM] * 3,
+        out_specs=(VMEM,) * 4,
+        scratch_shapes=[
+            pltpu.VMEM((tile_count, TILE, TILE), BF16),
+            pltpu.VMEM((row_count, 16, TILE), BF16),
+            pltpu.VMEM((cap, TILE), F32),
+        ],
+        compiler_params=params(20),
+        name="build",
+    )(count, rows, tiles, source_cells.T, target_cells.T, by_row)
+    kern = pltpu.with_memory_space_constraint(kern, pltpu.VMEM)
+    part = pltpu.VMEM((cap, TILE), F32)
+
+    def call(body, name, smem, vmem, out_rows, table_rows):
+        return pl.pallas_call(
+            body,
+            out_shape=array((out_rows, TILE), F32),
+            in_specs=[SMEM] * len(smem) + [VMEM] * len(vmem),
+            out_specs=VMEM,
+            scratch_shapes=[pltpu.VMEM((table_rows, TILE), F32), part],
+            compiler_params=params(12),
+            name=name,
+        )(*smem, *vmem)
+
+    first = sum_over_tgt(total)
+    cols = call(
+        first_col_kernel, "first_col", (count, rows), (first, log_rows, kern, by_tile), tile_count, row_count
+    )
+    cols = sum_over_src(cols)
+    second = call(row_kernel, "row", (count, tiles), (cols, log_cols, kern, by_row), row_count, tile_count)
+    second = sum_over_tgt(second)
+    cols = call(
+        next_col_kernel, "next_col", (count, rows), (second, first, log_rows, kern, by_tile), tile_count, row_count
+    )
+    cols = sum_over_src(cols)
+    source_pot = norm + EPS * log_rows - EPS * (jnp.log(second) + LN2 * shift)
+    target_pot = EPS * log_cols - EPS * jnp.log(cols)
+    return lax.cond(
+        jnp.max(cols) < POISONED,
+        lambda *unused: (source_pot.reshape(-1), target_pot.reshape(-1)),
+        general_path,
+        source_cells,
+        target_cells,
+        log_source,
+        log_target,
+        support,
+    )
+
+
 def solution(mesh):
     return jax.shard_map(
         on_device,

time: 1360 us -> 1510 us (1.11)
  starting transfers between devices: 0.16 us -> 50.9 us
  Pallas kernels: 0 us -> 43 us
  local copies, waits for them, and re-layouts: 83.3 us -> 124 us
  waiting for transfers between devices: 332 us -> 352 us
    ppermute x0 -> x20, starting transfers between devices: none -> 50.6 us  [the longest x18 50.4 us: moved(): return lax.ppermute(value, axis, [(i, perm(i, d)) for i in range(size)])]
    pallas_call x0 -> x5, Pallas kernels: none -> 43 us  [the longest x1 23.8 us: on_device(): pl.pallas_call(build_kernel, out_shape=(pltpu.VMEM((cap, TILE, TILE), BF1...]
    unnamed x15 -> x16, local copies, waits for them, and re-layouts: 2.19 us -> 42.7 us
    ppermute x0 -> x20, waiting for transfers between devices: none -> 21.5 us  [the longest x18 19.1 us: moved(): return lax.ppermute(value, axis, [(i, perm(i, d)) for i in range(size)])]
  transfers between devices with their start and end apart: 4 -> 24, of which waited for: 4 -> 15; matrix products, arithmetic and copies ran while one was open for 0% -> 0% of each run, Pallas kernels for 0% -> 0%
where the time goes in v1:
time: 1510 us
  other arithmetic  421 us (28%)
  matrix products  402 us (27%)
  waiting for transfers between devices  352 us (23%)
  local copies, waits for them, and re-layouts  124 us (8%)
  blocking collectives  95.6 us (6%)
  starting transfers between devices  50.9 us (3%)
  Pallas kernels  43 us (3%)
    dot_general x64, matrix products, cost_tile(): jnp.einsum('bie,bje->bij', src_block, tgt_block, preferred_element_type=j...  349 us
    psum x2, waiting for transfers between devices, across_targets(): return (highest, lax.psum(totals * jnp.exp(maxima - highest), 'tgt'))  168 us
    pmax x2, waiting for transfers between devices, across_targets(): highest = lax.pmax(maxima, 'tgt')  162 us
    reduce_sum x32, other arithmetic, exp_of(): terms = jnp.sum(jnp.exp(scores - slot_max[:, :, None]), axis=2)  144 us
    reduce_sum x32, other arithmetic, exp_of(): terms = jnp.sum(jnp.exp(scores - slot_max[:, None, :]), axis=1)  144 us
    reduce_max x64, other arithmetic, fold_block(): jnp.max(jnp.where(selector[:, :, None] > 0.5, block_max[:, None, :], NEG)...  111 us
    ppermute x18, starting transfers between devices, moved(): return lax.ppermute(value, axis, [(i, perm(i, d)) for i in range(size)])  50.4 us
    pmax x2, blocking collectives, across_sources(): highest = lax.pmax(maxima, 'src')  48.2 us
  transfers between devices with their start and end apart: 24, of which 15 were waited for; matrix products, arithmetic and copies ran while one was open for 0% of the time, Pallas kernels for 0%

profile of v1, /device:TPU:0, one launch (start us, length us, event | category | flops | bytes accessed | tf_op | source)
XLA Modules:
  0.0 1509.6 jit_solution(1171380870301918114)
XLA Ops:
  8.6 23.8 %build.1 = (bf16[1024,128,128]{2,1,0:T(8,128)(2,1)S(1)}, f32[256,128]{1,0:T(8,128)S(1)}, f32[256,128]{1,0:T(8,128)S(1)}, f32[256,128]{1,0:T(8,128)S(1)}) custom-call(s32[1,128]{1,0:T(1,128)S(1)} %get-tuple-element.290.count_ref, s32[1,1024]{1,0:T(1,128)S(1)} %get-tuple-element.291.rows_ref, s32[1,1024]{1,0:T(1,128)S(1)} %get-tuple-element.292.tiles_ref, ...), custom_call_target="tpu_custom_call" | custom-call | tf_op jit(solution)/shard_map/build/pallas_call | solution.py:474
  32.4 11.1 copy-done
  68.1 10.5 copy-done.1
  78.6 6.7 first_col.1
  86.6 7.1 collective-permute-start.7
  98.9 10.5 copy-done.2
  131.4 10.5 copy-done.3
  141.9 6.7 next_col.1
  150.0 10.1 collective-permute-start.17
  166.5 1336.6 %conditional.1 = (f32[32768]{0:T(1024)}, f32[8192]{0:T(1024)}) conditional(s32[]{:T(128)} %convert_element_type.59, (f32[32768]{0:T(1024)S(1)}, s32[256,32]{0,1:T(8,128)S(1)}, bf16[32768,64]{0,1:T(8,128)(2,1)}, bf16[8192,64]{0,1:T(8,128)(2,1)S(1)}, f32[8192]{0:T(1024)S(1)}) %tuple.188, (f32[256,128]{1,0:T(8,128)S(1)}, f32[256,128]{1,0:T(8,128)S(1)}, ...), branch_computations={%region_1.36_spmd, %region_36.37_spmd} | conditional | flops 801467648 | bytes 158626896 | solution.py:519
  167.7 5.6 copy_bitcast_fusion
  176.0 30.4 %scatter_custom_fusion = s32[1024]{0:T(1024)S(1)} fusion(s32[8192]{0:T(1024)S(1)} %bitcast.195, s32[8192]{0:T(1024)S(1)} %iota.59, s32[]{:T(128)} %constant.167.clone), kind=kCustom, calls=%fused_computation.224 | custom fusion | bytes 4100 | tf_op jit(solution)/shard_map/cond/branch_0_fun/scatter | solution.py:172
  206.5 6.2 gather_fusion
  212.7 13.5 gather_fusion.4
  229.0 15.7 %gather_fusion.3 = bf16[1024,128,64]{1,2,0:T(8,128)(2,1)} fusion(bf16[256,128,64]{1,2,0:T(8,128)(2,1)} %copy_bitcast_fusion, s32[1024]{0:T(1024)S(1)} %get-tuple-element.582), kind=kCustom, calls=%fused_computation.3 | custom fusion | bytes 33558528 | tf_op jit(solution)/shard_map/cond/branch_0_fun/gather | solution.py:179
  248.3 223.4 %while.48 = (s32[]{:T(128)}, f32[256,128]{1,0:T(8,128)S(1)}, f32[256,128]{1,0:T(8,128)S(1)}, s32[16,64]{1,0:T(8,128)S(1)}, pred[16,64]{1,0:T(8,128)(4,1)S(1)}, /...) while((s32[]{:T(128)}, f32[256,128]{1,0:T(8,128)S(1)}, ...), condition=%wide.region_12.12_spmd.clone, body=%wide.region_8.11_spmd.clone.sunk | while | flops 208982080 | bytes 12587404 | solution.py:98
  248.5 5.4 fusion.177
  262.5 5.4 fusion.177
  290.4 5.4 fusion.177
  304.4 5.4 fusion.177
  318.3 5.4 fusion.177
  332.3 5.4 fusion.177
  346.2 5.4 fusion.177
  360.2 5.4 fusion.177
  374.2 5.4 fusion.177
  388.1 5.4 fusion.177
  402.1 5.4 fusion.177
  416.1 5.4 fusion.177
  430.0 5.4 fusion.177
  444.0 5.4 fusion.177
  457.9 5.4 fusion.177
  472.4 83.1 %all-reduce.5.cloned.1.call-done = f32[256,128]{1,0:T(8,128)} async-done(((f32[256,128]{1,0:T(8,128)}), f32[256,128]{1,0:T(8,128)}) %all-reduce.5.cloned.1.call-update) | async-done | bytes 131088 | tf_op jit(solution)/shard_map/cond/branch_0_fun/pmax | solution.py:145
  557.2 84.0 %all-reduce.7.cloned.1.call-done = f32[256,128]{1,0:T(8,128)} async-done(((f32[256,128]{1,0:T(8,128)}), f32[256,128]{1,0:T(8,128)}) %all-reduce.7.cloned.1.call-update) | async-done | bytes 131088 | tf_op jit(solution)/shard_map/cond/branch_0_fun/psum | solution.py:146
  642.2 187.3 %while.49 = (s32[]{:T(128)}, f32[64,128]{1,0:T(8,128)S(1)}, f32[64,128]{1,0:T(8,128)S(1)}, s32[16,64]{1,0:T(8,128)S(1)}, pred[16,64]{1,0:T(8,128)(4,1)S(1)}, /*i...) while((s32[]{:T(128)}, f32[64,128]{1,0:T(8,128)S(1)}, ...), condition=%wide.region_19.19_spmd.clone, body=%wide.region_15.18_spmd.clone.sunk | while | flops 186740800 | bytes 11612564 | solution.py:141
  642.5 5.4 fusion.187
  665.9 5.4 fusion.187
  677.6 5.4 fusion.187
  689.3 5.4 fusion.187
  701.1 5.4 fusion.187
  712.8 5.4 fusion.187
  724.5 5.4 fusion.187
  736.2 5.4 fusion.187
  759.6 5.4 fusion.187
  783.0 5.4 fusion.187
  794.7 5.4 fusion.187
  818.1 5.4 fusion.187
  829.6 24.1 %pmax.25 = f32[64,128]{1,0:T(8,128)S(1)} all-reduce(f32[64,128]{1,0:T(8,128)S(1)} %get-tuple-element.267), channel_id=1, replica_groups=mesh['src'=8,'tgt'=16] {'src'}, use_global_device_ids=true, to_apply=%region_20.20 | all-reduce | flops 8192 | bytes 65536 | tf_op jit(solution)/shard_map/cond/branch_0_fun/pmax | solution.py:150
  853.7 23.8 %psum.25 = f32[64,128]{1,0:T(8,128)S(1)} all-reduce(f32[64,128]{1,0:T(8,128)S(1)} %exponential_multiply_fusion.3), channel_id=1, replica_groups=mesh['src'=8,'tgt'=16] {'src'}, use_global_device_ids=true, to_apply=%region_21.21 | all-reduce | flops 8192 | bytes 65536 | tf_op jit(solution)/shard_map/cond/branch_0_fun/psum | solution.py:151
  877.5 223.4 %while.50 = (s32[]{:T(128)}, f32[256,128]{1,0:T(8,128)S(1)}, f32[256,128]{1,0:T(8,128)S(1)}, s32[16,64]{1,0:T(8,128)S(1)}, pred[16,64]{1,0:T(8,128)(4,1)S(1)}, /...) while((s32[]{:T(128)}, f32[256,128]{1,0:T(8,128)S(1)}, ...), condition=%wide.region_26.26_spmd.clone, body=%wide.region_22.25_spmd.clone.sunk | while | flops 208982080 | bytes 12620180 | solution.py:98
  1101.6 79.1 %all-reduce.9.cloned.1.call-done = f32[256,128]{1,0:T(8,128)} async-done(((f32[256,128]{1,0:T(8,128)}), f32[256,128]{1,0:T(8,128)}) %all-reduce.9.cloned.1.call-update) | async-done | bytes 131088 | tf_op jit(solution)/shard_map/cond/branch_0_fun/pmax | solution.py:145
  1182.5 84.0 %all-reduce.11.cloned.1.call-done = f32[256,128]{1,0:T(8,128)} async-done(((f32[256,128]{1,0:T(8,128)}), f32[256,128]{1,0:T(8,128)}) %all-reduce.11.cloned.1.call-update) | async-done | bytes 131088 | tf_op jit(solution)/shard_map/cond/branch_0_fun/psum | solution.py:146
  1267.4 187.3 %while.51 = (s32[]{:T(128)}, f32[64,128]{1,0:T(8,128)S(1)}, f32[64,128]{1,0:T(8,128)S(1)}, s32[16,64]{1,0:T(8,128)S(1)}, pred[16,64]{1,0:T(8,128)(4,1)S(1)}, /*i...) while((s32[]{:T(128)}, f32[64,128]{1,0:T(8,128)S(1)}, ...), condition=%wide.region_33.33_spmd.clone, body=%wide.region_29.32_spmd.clone.sunk | while | flops 186740800 | bytes 11612564 | solution.py:141
  1267.7 5.4 fusion.207
  1279.4 5.4 fusion.207
  1302.8 5.4 fusion.207
  1326.2 5.4 fusion.207
  1338.0 5.4 fusion.207
  1361.4 5.4 fusion.207
  1384.8 5.4 fusion.207
  1396.5 5.4 fusion.207
  1419.9 5.4 fusion.207
  1443.3 5.4 fusion.207
  1454.8 24.1 %pmax.27 = f32[64,128]{1,0:T(8,128)S(1)} all-reduce(f32[64,128]{1,0:T(8,128)S(1)} %get-tuple-element.271), channel_id=1, replica_groups=mesh['src'=8,'tgt'=16] {'src'}, use_global_device_ids=true, to_apply=%region_34.34 | all-reduce | flops 8192 | bytes 65536 | tf_op jit(solution)/shard_map/cond/branch_0_fun/pmax | solution.py:150
  1478.9 23.6 %psum.27 = f32[64,128]{1,0:T(8,128)S(1)} all-reduce(f32[64,128]{1,0:T(8,128)S(1)} %exponential_multiply_fusion.2), channel_id=1, replica_groups=mesh['src'=8,'tgt'=16] {'src'}, use_global_device_ids=true, to_apply=%region_35.35 | all-reduce | flops 8192 | bytes 65536 | tf_op jit(solution)/shard_map/cond/branch_0_fun/psum | solution.py:151
  (912 shorter events, 692.9 us)
Async XLA Ops:
  7.2 60.9 %copy-start.9 = (f32[32768]{0:T(1024)S(1)}, f32[32768]{0:T(1024)}, u32[]{:S(2)}) copy-start(f32[32768]{0:T(1024)} %param.17) | copy-start | bytes 393220
  32.4 11.1 copy-start
  43.5 7.4 collective-permute-start
  46.6 6.6 collective-permute-start.1
  47.2 6.0 collective-permute-start.2
  53.3 10.8 collective-permute-start.3
  56.8 11.2 collective-permute-start.4
  61.4 6.6 collective-permute-start.5
  68.1 10.5 copy-start.1
  78.6 20.2 %copy-start.10 = (f32[8192]{0:T(1024)S(1)}, f32[8192]{0:T(1024)}, u32[]{:S(2)}) copy-start(f32[8192]{0:T(1024)} %param.18) | copy-start | bytes 98308
  85.3 1.3 collective-permute-start.6
  86.6 10.3 collective-permute-start.7
  93.7 5.1 collective-permute-start.8
  93.7 5.1 collective-permute-start.9
  98.8 10.5 copy-start.2
  113.7 7.2 collective-permute-start.10
  113.8 8.4 collective-permute-start.11
  115.0 7.1 collective-permute-start.12
  122.2 7.5 collective-permute-start.13
  123.0 8.4 collective-permute-start.14
  126.2 5.2 collective-permute-start.15
  131.4 10.5 copy-start.3
  141.9 24.5 %copy-start.7 = (bf16[8192,64]{0,1:T(8,128)(2,1)S(1)}, bf16[8192,64]{0,1:T(8,128)(2,1)}, u32[]{:S(2)}) copy-start(bf16[8192,64]{0,1:T(8,128)(2,1)} %param.16) | copy-start | bytes 3145732
  141.9 24.5 %copy-start.11 = (s32[256,32]{0,1:T(8,128)S(1)}, s32[256,32]{0,1:T(8,128)}, u32[]{:S(2)}) copy-start(s32[256,32]{0,1:T(8,128)} %param.19) | copy-start | bytes 98308
  148.7 1.3 collective-permute-start.16
  150.0 13.3 collective-permute-start.17
  160.1 5.1 collective-permute-start.18
  160.1 5.1 collective-permute-start.19
  166.5 389.0 %all-reduce.5.cloned.1.call-start = ((), (), s32[]{:S(2)}) async-start(), calls=%async_computation | async-start | bytes 262144 | tf_op jit(solution)/shard_map/cond/branch_0_fun/pmax | solution.py:145
  167.7 5.6 copy-start.4
  471.6 0.7 copy-start.6
  472.3 168.9 %all-reduce.7.cloned.1.call-start = ((), (), s32[]{:S(2)}) async-start(), calls=%async_computation.1 | async-start | bytes 262144 | tf_op jit(solution)/shard_map/cond/branch_0_fun/psum | solution.py:146
  557.1 623.6 %all-reduce.9.cloned.1.call-start = ((), (), s32[]{:S(2)}) async-start(), calls=%async_computation.2 | async-start | bytes 262144 | tf_op jit(solution)/shard_map/cond/branch_0_fun/pmax | solution.py:145
  1100.9 0.7 copy-start.5
  1101.6 164.8 %all-reduce.11.cloned.1.call-start = ((), (), s32[]{:S(2)}) async-start(), calls=%async_computation.3 | async-start | bytes 262144 | tf_op jit(solution)/shard_map/cond/branch_0_fun/psum | solution.py:146
  1454.8 48.3 %copy-start.8 = (f32[256,128]{1,0:T(8,128)}, f32[256,128]{1,0:T(8,128)S(1)}, u32[]{:S(2)}) copy-start(f32[256,128]{1,0:T(8,128)S(1)} %get-tuple-element.1090) | copy-start | bytes 393220 | tf_op jit(solution)/shard_map/cond
Sparse Core Ops, SparseCore 0:
  472.4 82.9 all-reduce.4
  559.5 81.6 all-reduce.6
  1101.7 78.9 all-reduce.8
  1184.7 81.6 all-reduce.10

commit v2 on v1

--- a/solution.py
+++ b/solution.py
@@ -222,6 +222,7 @@
 COL_UNROLL = 64
 SMEM = pl.BlockSpec(memory_space=pltpu.SMEM)
 VMEM = pl.BlockSpec(memory_space=pltpu.VMEM)
+ANY = pl.BlockSpec(memory_space=pl.ANY)
 BF16 = jnp.bfloat16
 F32 = jnp.float32
 
@@ -246,11 +247,11 @@
     return lax.broadcasted_iota(jnp.int32, shape, axis)
 
 
-def list_kernel(place_ref, sup_ref, rows_ref, tiles_ref, count_ref, by_row_ref, by_tile_ref):
+def list_support(sup_ref, rows_ref, tiles_ref, count_ref, by_row_ref, by_tile_ref):
     width, rows = sup_ref.shape
     cap = rows_ref.shape[1]
     own_tiles = by_tile_ref.shape[0]
-    local = sup_ref[...] - place_ref[0] * own_tiles
+    local = sup_ref[...] - lax.axis_index("tgt") * own_tiles
     owned = (local >= 0) & (local < own_tiles)
     mask = ones_where(owned)
     lower = ones_where(iota((width, width), 1) <= iota((width, width), 0))
@@ -292,10 +293,30 @@
 
 
 def build_kernel(
-    count_ref, rows_ref, tiles_ref, src_ref, tgt_ref, by_row_ref,
-    kern_ref, sum_ref, norm_ref, shift_ref,
-    left, extra, part,
+    sup_hbm, src_hbm, tgt_hbm,
+    kern_ref, sum_ref, norm_ref, shift_ref, rows_out, tiles_out, count_out, by_row_ref, by_tile_ref,
+    left, extra, part, sup_ref, src_ref, tgt_ref, rows_ref, tiles_ref, count_ref, sems,
 ):
+    moves = [
+        pltpu.make_async_copy(*pair, sems.at[i])
+        for i, pair in enumerate(
+            [
+                (sup_hbm, sup_ref),
+                (tgt_hbm, tgt_ref),
+                (src_hbm, src_ref),
+                (rows_out, rows_ref),
+                (tiles_out, tiles_ref),
+                (count_out, count_ref),
+            ]
+        )
+    ]
+    for move in moves[:3]:
+        move.start()
+    moves[0].wait()
+    list_support(sup_ref, rows_out, tiles_out, count_out, by_row_ref, by_tile_ref)
+    for move in moves[3:]:
+        move.start()
+    moves[1].wait()
     dim, tgt_count = tgt_ref.shape
     row_count = extra.shape[0]
     lane = iota((TILE, TILE), 1)
@@ -313,6 +334,7 @@
 
     lax.fori_loop(0, tgt_count // TILE, one_tgt, 0)
     line = iota((16, TILE), 0)
+    moves[2].wait()
 
     def one_src(r, unused):
         block = src_ref[:, pl.ds(pl.multiple_of(r * TILE, TILE), TILE)].astype(F32)
@@ -325,6 +347,8 @@
 
     lax.fori_loop(0, row_count, one_src, 0, unroll=8)
     part[...] = jnp.zeros_like(part)
+    for move in moves[3:]:
+        move.wait()
     pad = jnp.zeros((TILE - dim - 16, TILE), BF16)
 
     def step(g, unused):
@@ -363,10 +387,19 @@
     ).astype(BF16)
 
 
-def row_kernel(count_ref, tiles_ref, total_ref, log_ref, kern_ref, by_row_ref, out_ref, table, part):
+def start(log_hbm, log_ref, sem, total, table, part):
+    move = pltpu.make_async_copy(log_hbm, log_ref, sem)
+    move.start()
+    part[...] = jnp.zeros_like(part)
+    move.wait()
+    table[...] = jnp.exp(log_ref[...]) / total
+
+
+def row_kernel(
+    kern_ref, count_ref, tiles_ref, log_hbm, total_ref, by_row_ref, out_ref, table, part, log_ref, sem
+):
     total = total_ref[...]
-    table[...] = jnp.exp(log_ref[...]) / total
-    part[...] = jnp.zeros_like(part)
+    start(log_hbm, log_ref, sem, total, table, part)
 
     def step(g, unused):
         base = g * ROW_UNROLL
@@ -384,9 +417,8 @@
     out_ref[...] = poison(in_range(total, COL_LOW, COL_HIGH), out)
 
 
-def col_body(ok, count_ref, rows_ref, total, log_ref, kern_ref, by_tile_ref, out_ref, table, part):
-    table[...] = jnp.exp(log_ref[...]) / total
-    part[...] = jnp.zeros_like(part)
+def col_body(ok, kern_ref, count_ref, rows_ref, total, by_tile_ref, out_ref, table, part, log_hbm, log_ref, sem):
+    start(log_hbm, log_ref, sem, total, table, part)
     none = jnp.zeros((16, TILE), BF16)
 
     def step(g, unused):
@@ -416,19 +448,21 @@
     out_ref[...] = poison(ok, sum_slots(by_tile_ref[...], part[...]))
 
 
-def first_col_kernel(count_ref, rows_ref, total_ref, log_ref, kern_ref, by_tile_ref, out_ref, table, part):
+def first_col_kernel(
+    kern_ref, count_ref, rows_ref, log_hbm, total_ref, by_tile_ref, out_ref, table, part, log_ref, sem
+):
     total = total_ref[...]
     ok = in_range(total, ROW_LOW, ROW_HIGH)
-    col_body(ok, count_ref, rows_ref, total, log_ref, kern_ref, by_tile_ref, out_ref, table, part)
+    col_body(ok, kern_ref, count_ref, rows_ref, total, by_tile_ref, out_ref, table, part, log_hbm, log_ref, sem)
 
 
 def next_col_kernel(
-    count_ref, rows_ref, total_ref, earlier_ref, log_ref, kern_ref, by_tile_ref, out_ref, table, part
+    kern_ref, count_ref, rows_ref, log_hbm, total_ref, earlier_ref, by_tile_ref, out_ref, table, part, log_ref, sem
 ):
     total = total_ref[...]
     ratio = total / earlier_ref[...]
     ok = in_range(total, ROW_LOW, ROW_HIGH) & in_range(ratio, 1.0 / RATIO, RATIO)
-    col_body(ok, count_ref, rows_ref, total, log_ref, kern_ref, by_tile_ref, out_ref, table, part)
+    col_body(ok, kern_ref, count_ref, rows_ref, total, by_tile_ref, out_ref, table, part, log_hbm, log_ref, sem)
 
 
 def ring_sum(value, axis, size, perm):
@@ -453,65 +487,64 @@
     row_count = source_cells.shape[0] // TILE
     tile_count = target_cells.shape[0] // TILE
     cap = 2 * support.size // lax.axis_size("tgt")
-    place = lax.axis_index("tgt").astype(jnp.int32).reshape(1)
     log_rows = log_source.reshape(row_count, TILE)
     log_cols = log_target.reshape(tile_count, TILE)
     array = jax.ShapeDtypeStruct
-    rows, tiles, count, by_row, by_tile = pl.pallas_call(
-        list_kernel,
+    kern, total, norm, shift, rows, tiles, count, by_row, by_tile = pl.pallas_call(
+        build_kernel,
         out_shape=(
+            pltpu.VMEM((cap, TILE, TILE), BF16),
+            array((row_count, TILE), F32),
+            array((row_count, TILE), F32),
+            array((row_count, TILE), F32),
             array((1, cap), jnp.int32),
             array((1, cap), jnp.int32),
             array((1, TILE), jnp.int32),
             array((row_count, cap), BF16),
             array((tile_count, cap), BF16),
         ),
-        in_specs=[SMEM, VMEM],
-        out_specs=(VMEM,) * 5,
-        compiler_params=params(16),
-        name="list_support",
-    )(place, support.T)
-    kern, total, norm, shift = pl.pallas_call(
-        build_kernel,
-        out_shape=(
-            pltpu.VMEM((cap, TILE, TILE), BF16),
-            array((row_count, TILE), F32),
-            array((row_count, TILE), F32),
-            array((row_count, TILE), F32),
-        ),
-        in_specs=[SMEM] * 3 + [VMEM] * 3,
-        out_specs=(VMEM,) * 4,
+        in_specs=[ANY] * 3,
+        out_specs=(VMEM,) * 9,
         scratch_shapes=[
             pltpu.VMEM((tile_count, TILE, TILE), BF16),
             pltpu.VMEM((row_count, 16, TILE), BF16),
             pltpu.VMEM((cap, TILE), F32),
+            pltpu.VMEM(support.shape[::-1], jnp.int32),
+            pltpu.VMEM(source_cells.shape[::-1], BF16),
+            pltpu.VMEM(target_cells.shape[::-1], BF16),
+            pltpu.SMEM((1, cap), jnp.int32),
+            pltpu.SMEM((1, cap), jnp.int32),
+            pltpu.SMEM((1, TILE), jnp.int32),
+            pltpu.SemaphoreType.DMA((6,)),
         ],
         compiler_params=params(20),
         name="build",
-    )(count, rows, tiles, source_cells.T, target_cells.T, by_row)
+    )(support.T, source_cells.T, target_cells.T)
     kern = pltpu.with_memory_space_constraint(kern, pltpu.VMEM)
-    part = pltpu.VMEM((cap, TILE), F32)
-
-    def call(body, name, smem, vmem, out_rows, table_rows):
+
+    def call(body, name, slots, log, vmem, out_rows, table_rows):
         return pl.pallas_call(
             body,
             out_shape=array((out_rows, TILE), F32),
-            in_specs=[SMEM] * len(smem) + [VMEM] * len(vmem),
+            in_specs=[VMEM, SMEM, SMEM, ANY] + [VMEM] * len(vmem),
             out_specs=VMEM,
-            scratch_shapes=[pltpu.VMEM((table_rows, TILE), F32), part],
-            compiler_params=params(12),
+            scratch_shapes=[
+                pltpu.VMEM((table_rows, TILE), F32),
+                pltpu.VMEM((cap, TILE), F32),
+                pltpu.VMEM((table_rows, TILE), F32),
+                pltpu.SemaphoreType.DMA,
+            ],
+            compiler_params=params(20),
             name=name,
-        )(*smem, *vmem)
+        )(kern, count, slots, log, *vmem)
 
     first = sum_over_tgt(total)
-    cols = call(
-        first_col_kernel, "first_col", (count, rows), (first, log_rows, kern, by_tile), tile_count, row_count
-    )
+    cols = call(first_col_kernel, "first_col", rows, log_rows, (first, by_tile), tile_count, row_count)
     cols = sum_over_src(cols)
-    second = call(row_kernel, "row", (count, tiles), (cols, log_cols, kern, by_row), row_count, tile_count)
+    second = call(row_kernel, "row", tiles, log_cols, (cols, by_row), row_count, tile_count)
     second = sum_over_tgt(second)
     cols = call(
-        next_col_kernel, "next_col", (count, rows), (second, first, log_rows, kern, by_tile), tile_count, row_count
+        next_col_kernel, "next_col", rows, log_rows, (second, first, by_tile), tile_count, row_count
     )
     cols = sum_over_src(cols)
     source_pot = norm + EPS * log_rows - EPS * (jnp.log(second) + LN2 * shift)

time: 1510 us -> 1470 us (0.974)
  local copies, waits for them, and re-layouts: 124 us -> 81.4 us
    unnamed x16 -> x8, local copies, waits for them, and re-layouts: 42.7 us -> 0.02 us
  transfers between devices with their start and end apart: 24 -> 24, of which waited for: 15 -> 17; matrix products, arithmetic and copies ran while one was open for 0% -> 0% of each run, Pallas kernels for 0% -> 0%
where the time goes in v2:
time: 1470 us
  other arithmetic  421 us (29%)
  matrix products  402 us (27%)
  waiting for transfers between devices  355 us (24%)
  blocking collectives  95.6 us (7%)
  local copies, waits for them, and re-layouts  81.4 us (6%)
  starting transfers between devices  47.5 us (3%)
  Pallas kernels  41 us (3%)
    dot_general x64, matrix products, cost_tile(): jnp.einsum('bie,bje->bij', src_block, tgt_block, preferred_element_type=j...  349 us
    psum x2, waiting for transfers between devices, across_targets(): return (highest, lax.psum(totals * jnp.exp(maxima - highest), 'tgt'))  168 us
    pmax x2, waiting for transfers between devices, across_targets(): highest = lax.pmax(maxima, 'tgt')  167 us
    reduce_sum x32, other arithmetic, exp_of(): terms = jnp.sum(jnp.exp(scores - slot_max[:, :, None]), axis=2)  144 us
    reduce_sum x32, other arithmetic, exp_of(): terms = jnp.sum(jnp.exp(scores - slot_max[:, None, :]), axis=1)  144 us
    reduce_max x64, other arithmetic, fold_block(): jnp.max(jnp.where(selector[:, :, None] > 0.5, block_max[:, None, :], NEG)...  111 us
    pmax x2, blocking collectives, across_sources(): highest = lax.pmax(maxima, 'src')  48.2 us
    psum x2, blocking collectives, across_sources(): return (highest, lax.psum(totals * jnp.exp(maxima - highest), 'src'))  47.4 us
  transfers between devices with their start and end apart: 24, of which 17 were waited for; matrix products, arithmetic and copies ran while one was open for 0% of the time, Pallas kernels for 0%

profile of v2, /device:TPU:0, one launch (start us, length us, event | category | flops | bytes accessed | tf_op | source)
XLA Modules:
  0.0 1465.2 jit_solution(12543236664031762799)
XLA Ops:
  7.2 22.9 %build.1 = (bf16[1024,128,128]{2,1,0:T(8,128)(2,1)S(1)}, f32[256,128]{1,0:T(8,128)S(1)}, f32[256,128]{1,0:T(8,128)S(1)}, f32[256,128]{1,0:T(8,128)S(1)}, s32[1,1...) custom-call(s32[32,256]{1,0:T(8,128)} %bitcast.191, ...), custom_call_target="tpu_custom_call" | custom-call | tf_op jit(solution)/shard_map/build/pallas_call | solution.py:493
  39.9 7.9 collective-permute-start.3
  54.1 6.9 first_col.1
  98.1 6.9 next_col.1
  117.3 1341.4 %conditional.1 = (f32[32768]{0:T(1024)}, f32[8192]{0:T(1024)}) conditional(s32[]{:T(128)} %convert_element_type.59, (f32[32768]{0:T(1024)S(1)}, s32[256,32]{0,1:T(8,128)S(1)}, bf16[32768,64]{0,1:T(8,128)(2,1)}, bf16[8192,64]{0,1:T(8,128)(2,1)S(1)}, f32[8192]{0:T(1024)S(1)}) %tuple.188, (f32[256,128]{1,0:T(8,128)S(1)}, f32[256,128]{1,0:T(8,128)S(1)}, ...), branch_computations={%region_1.36_spmd, %region_36.37_spmd} | conditional | flops 801467648 | bytes 158626896 | solution.py:552
  118.6 5.6 copy_bitcast_fusion
  126.8 30.4 %scatter_custom_fusion = s32[1024]{0:T(1024)S(1)} fusion(s32[8192]{0:T(1024)S(1)} %bitcast.194, s32[8192]{0:T(1024)S(1)} %iota.59, s32[]{:T(128)} %constant.164.clone), kind=kCustom, calls=%fused_computation.224 | custom fusion | bytes 4100 | tf_op jit(solution)/shard_map/cond/branch_0_fun/scatter | solution.py:172
  157.3 6.2 gather_fusion
  163.6 13.5 gather_fusion.4
  179.8 15.7 %gather_fusion.3 = bf16[1024,128,64]{1,2,0:T(8,128)(2,1)} fusion(bf16[256,128,64]{1,2,0:T(8,128)(2,1)} %copy_bitcast_fusion, s32[1024]{0:T(1024)S(1)} %get-tuple-element.582), kind=kCustom, calls=%fused_computation.3 | custom fusion | bytes 33558528 | tf_op jit(solution)/shard_map/cond/branch_0_fun/gather | solution.py:179
  199.1 223.4 %while.48 = (s32[]{:T(128)}, f32[256,128]{1,0:T(8,128)S(1)}, f32[256,128]{1,0:T(8,128)S(1)}, s32[16,64]{1,0:T(8,128)S(1)}, pred[16,64]{1,0:T(8,128)(4,1)S(1)}, /...) while((s32[]{:T(128)}, f32[256,128]{1,0:T(8,128)S(1)}, ...), condition=%wide.region_12.12_spmd.clone, body=%wide.region_8.11_spmd.clone.sunk | while | flops 208982080 | bytes 12587404 | solution.py:98
  227.3 5.4 fusion.177
  241.2 5.4 fusion.177
  255.2 5.4 fusion.177
  269.2 5.4 fusion.177
  283.1 5.4 fusion.177
  297.1 5.4 fusion.177
  311.0 5.4 fusion.177
  325.0 5.4 fusion.177
  339.0 5.4 fusion.177
  352.9 5.4 fusion.177
  366.9 5.4 fusion.177
  380.9 5.4 fusion.177
  394.8 5.4 fusion.177
  408.8 5.4 fusion.177
  423.2 87.8 %all-reduce.5.cloned.1.call-done = f32[256,128]{1,0:T(8,128)} async-done(((f32[256,128]{1,0:T(8,128)}), f32[256,128]{1,0:T(8,128)}) %all-reduce.5.cloned.1.call-update) | async-done | bytes 131088 | tf_op jit(solution)/shard_map/cond/branch_0_fun/pmax | solution.py:145
  512.8 84.0 %all-reduce.7.cloned.1.call-done = f32[256,128]{1,0:T(8,128)} async-done(((f32[256,128]{1,0:T(8,128)}), f32[256,128]{1,0:T(8,128)}) %all-reduce.7.cloned.1.call-update) | async-done | bytes 131088 | tf_op jit(solution)/shard_map/cond/branch_0_fun/psum | solution.py:146
  597.8 187.3 %while.49 = (s32[]{:T(128)}, f32[64,128]{1,0:T(8,128)S(1)}, f32[64,128]{1,0:T(8,128)S(1)}, s32[16,64]{1,0:T(8,128)S(1)}, pred[16,64]{1,0:T(8,128)(4,1)S(1)}, /*i...) while((s32[]{:T(128)}, f32[64,128]{1,0:T(8,128)S(1)}, ...), condition=%wide.region_19.19_spmd.clone, body=%wide.region_15.18_spmd.clone.sunk | while | flops 186740800 | bytes 11612564 | solution.py:141
  609.8 5.4 fusion.187
  621.5 5.4 fusion.187
  633.2 5.4 fusion.187
  644.9 5.4 fusion.187
  656.6 5.4 fusion.187
  668.3 5.4 fusion.187
  680.0 5.4 fusion.187
  691.7 5.4 fusion.187
  703.5 5.4 fusion.187
  715.2 5.4 fusion.187
  726.9 5.4 fusion.187
  738.6 5.4 fusion.187
  750.3 5.4 fusion.187
  762.0 5.4 fusion.187
  773.7 5.4 fusion.187
  785.1 24.1 %pmax.25 = f32[64,128]{1,0:T(8,128)S(1)} all-reduce(f32[64,128]{1,0:T(8,128)S(1)} %get-tuple-element.267), channel_id=1, replica_groups=mesh['src'=8,'tgt'=16] {'src'}, use_global_device_ids=true, to_apply=%region_20.20 | all-reduce | flops 8192 | bytes 65536 | tf_op jit(solution)/shard_map/cond/branch_0_fun/pmax | solution.py:150
  809.2 23.8 %psum.25 = f32[64,128]{1,0:T(8,128)S(1)} all-reduce(f32[64,128]{1,0:T(8,128)S(1)} %exponential_multiply_fusion.3), channel_id=1, replica_groups=mesh['src'=8,'tgt'=16] {'src'}, use_global_device_ids=true, to_apply=%region_21.21 | all-reduce | flops 8192 | bytes 65536 | tf_op jit(solution)/shard_map/cond/branch_0_fun/psum | solution.py:151
  833.1 223.4 %while.50 = (s32[]{:T(128)}, f32[256,128]{1,0:T(8,128)S(1)}, f32[256,128]{1,0:T(8,128)S(1)}, s32[16,64]{1,0:T(8,128)S(1)}, pred[16,64]{1,0:T(8,128)(4,1)S(1)}, /...) while((s32[]{:T(128)}, f32[256,128]{1,0:T(8,128)S(1)}, ...), condition=%wide.region_26.26_spmd.clone, body=%wide.region_22.25_spmd.clone.sunk | while | flops 208982080 | bytes 12620180 | solution.py:98
  833.3 5.4 fusion.197
  847.3 5.4 fusion.197
  861.3 5.4 fusion.197
  889.2 5.4 fusion.197
  1057.2 79.1 %all-reduce.9.cloned.1.call-done = f32[256,128]{1,0:T(8,128)} async-done(((f32[256,128]{1,0:T(8,128)}), f32[256,128]{1,0:T(8,128)}) %all-reduce.9.cloned.1.call-update) | async-done | bytes 131088 | tf_op jit(solution)/shard_map/cond/branch_0_fun/pmax | solution.py:145
  1138.0 84.0 %all-reduce.11.cloned.1.call-done = f32[256,128]{1,0:T(8,128)} async-done(((f32[256,128]{1,0:T(8,128)}), f32[256,128]{1,0:T(8,128)}) %all-reduce.11.cloned.1.call-update) | async-done | bytes 131088 | tf_op jit(solution)/shard_map/cond/branch_0_fun/psum | solution.py:146
  1223.0 187.3 %while.51 = (s32[]{:T(128)}, f32[64,128]{1,0:T(8,128)S(1)}, f32[64,128]{1,0:T(8,128)S(1)}, s32[16,64]{1,0:T(8,128)S(1)}, pred[16,64]{1,0:T(8,128)(4,1)S(1)}, /*i...) while((s32[]{:T(128)}, f32[64,128]{1,0:T(8,128)S(1)}, ...), condition=%wide.region_33.33_spmd.clone, body=%wide.region_29.32_spmd.clone.sunk | while | flops 186740800 | bytes 11612564 | solution.py:141
  1235.0 5.4 fusion.207
  1246.7 5.4 fusion.207
  1270.1 5.4 fusion.207
  1293.5 5.4 fusion.207
  1305.2 5.4 fusion.207
  1328.6 5.4 fusion.207
  1352.1 5.4 fusion.207
  1363.8 5.4 fusion.207
  1387.2 5.4 fusion.207
  1410.3 24.1 %pmax.27 = f32[64,128]{1,0:T(8,128)S(1)} all-reduce(f32[64,128]{1,0:T(8,128)S(1)} %get-tuple-element.271), channel_id=1, replica_groups=mesh['src'=8,'tgt'=16] {'src'}, use_global_device_ids=true, to_apply=%region_34.34 | all-reduce | flops 8192 | bytes 65536 | tf_op jit(solution)/shard_map/cond/branch_0_fun/pmax | solution.py:150
  1434.4 23.6 %psum.27 = f32[64,128]{1,0:T(8,128)S(1)} all-reduce(f32[64,128]{1,0:T(8,128)S(1)} %exponential_multiply_fusion.2), channel_id=1, replica_groups=mesh['src'=8,'tgt'=16] {'src'}, use_global_device_ids=true, to_apply=%region_35.35 | all-reduce | flops 8192 | bytes 65536 | tf_op jit(solution)/shard_map/cond/branch_0_fun/psum | solution.py:151
  (903 shorter events, 668.9 us)
Async XLA Ops:
  7.2 46.9 %copy-start.5 = (f32[32768]{0:T(1024)S(1)}, f32[32768]{0:T(1024)}, u32[]{:S(2)}) copy-start(f32[32768]{0:T(1024)} %param.17) | copy-start | bytes 393220
  30.1 7.5 collective-permute-start
  33.2 6.7 collective-permute-start.1
  33.8 6.1 collective-permute-start.2
  39.9 12.1 collective-permute-start.3
  47.8 6.2 collective-permute-start.4
  47.8 6.2 collective-permute-start.5
  54.0 17.9 %copy-start.6 = (f32[8192]{0:T(1024)S(1)}, f32[8192]{0:T(1024)}, u32[]{:S(2)}) copy-start(f32[8192]{0:T(1024)} %param.18) | copy-start | bytes 98308
  61.0 1.3 collective-permute-start.6
  62.3 7.7 collective-permute-start.7
  66.8 5.1 collective-permute-start.8
  66.8 5.1 collective-permute-start.9
  76.2 6.7 collective-permute-start.10
  77.0 8.6 collective-permute-start.11
  79.2 6.4 collective-permute-start.12
  85.6 9.4 collective-permute-start.13
  90.7 6.2 collective-permute-start.14
  93.0 5.0 collective-permute-start.15
  98.0 19.3 %copy-start.3 = (bf16[8192,64]{0,1:T(8,128)(2,1)S(1)}, bf16[8192,64]{0,1:T(8,128)(2,1)}, u32[]{:S(2)}) copy-start(bf16[8192,64]{0,1:T(8,128)(2,1)} %param.16) | copy-start | bytes 3145732
  98.0 19.3 %copy-start.7 = (s32[256,32]{0,1:T(8,128)S(1)}, s32[256,32]{0,1:T(8,128)}, u32[]{:S(2)}) copy-start(s32[256,32]{0,1:T(8,128)} %param.19) | copy-start | bytes 98308
  105.0 1.3 collective-permute-start.16
  106.3 7.9 collective-permute-start.17
  110.9 5.1 collective-permute-start.18
  110.9 5.1 collective-permute-start.19
  117.3 393.7 %all-reduce.5.cloned.1.call-start = ((), (), s32[]{:S(2)}) async-start(), calls=%async_computation | async-start | bytes 262144 | tf_op jit(solution)/shard_map/cond/branch_0_fun/pmax | solution.py:145
  118.5 5.6 copy-start
  422.5 0.7 copy-start.2
  423.2 173.6 %all-reduce.7.cloned.1.call-start = ((), (), s32[]{:S(2)}) async-start(), calls=%async_computation.1 | async-start | bytes 262144 | tf_op jit(solution)/shard_map/cond/branch_0_fun/psum | solution.py:146
  512.7 623.6 %all-reduce.9.cloned.1.call-start = ((), (), s32[]{:S(2)}) async-start(), calls=%async_computation.2 | async-start | bytes 262144 | tf_op jit(solution)/shard_map/cond/branch_0_fun/pmax | solution.py:145
  1056.5 0.7 copy-start.1
  1057.2 164.8 %all-reduce.11.cloned.1.call-start = ((), (), s32[]{:S(2)}) async-start(), calls=%async_computation.3 | async-start | bytes 262144 | tf_op jit(solution)/shard_map/cond/branch_0_fun/psum | solution.py:146
  1410.3 48.3 %copy-start.4 = (f32[256,128]{1,0:T(8,128)}, f32[256,128]{1,0:T(8,128)S(1)}, u32[]{:S(2)}) copy-start(f32[256,128]{1,0:T(8,128)S(1)} %get-tuple-element.1090) | copy-start | bytes 393220 | tf_op jit(solution)/shard_map/cond
Sparse Core Ops, SparseCore 0:
  423.3 87.6 all-reduce.4
  515.1 81.6 all-reduce.6
  1057.3 78.9 all-reduce.8
  1140.3 81.6 all-reduce.10

commit v3 on v2

--- a/solution.py
+++ b/solution.py
@@ -18,11 +18,11 @@
 SCALE = 14.426950408889634
 LN2 = 0.6931471805599453
 SHIFT = 9.0
-ROW_LOW = 2.0**-30
+ROW_LOW = 2.0**-24
 ROW_HIGH = 2.0**80
-COL_LOW = 2.0**-10
+COL_LOW = 2.0**-40
 COL_HIGH = 2.0**80
-RATIO = 2.0**30
+RATIO = 2.0**20
 POISON = 3.0e38
 POISONED = 1.0e37
 
@@ -217,9 +217,10 @@
 
 
 CAP_STEP = 128
-BUILD_UNROLL = 64
-ROW_UNROLL = 64
-COL_UNROLL = 64
+BUILD_UNROLL = 128
+ROW_UNROLL = 128
+GROUP = 8
+GROUP_UNROLL = 16
 SMEM = pl.BlockSpec(memory_space=pltpu.SMEM)
 VMEM = pl.BlockSpec(memory_space=pltpu.VMEM)
 ANY = pl.BlockSpec(memory_space=pl.ANY)
@@ -247,10 +248,10 @@
     return lax.broadcasted_iota(jnp.int32, shape, axis)
 
 
-def list_support(sup_ref, rows_ref, tiles_ref, count_ref, by_row_ref, by_tile_ref):
+def list_support(sup_ref, tiles_ref, count_ref, rows_ref, by_row_ref, slots_ref, owners_ref, by_group_ref):
     width, rows = sup_ref.shape
     cap = rows_ref.shape[1]
-    own_tiles = by_tile_ref.shape[0]
+    own_tiles, groups = by_group_ref.shape
     local = sup_ref[...] - lax.axis_index("tgt") * own_tiles
     owned = (local >= 0) & (local < own_tiles)
     mask = ones_where(owned)
@@ -280,10 +281,35 @@
     tiles_ref[...] = tiles.astype(jnp.int32)
     rows_ref[...] = got[2 * width : 2 * width + 1].astype(jnp.int32)
     total = jnp.sum(count, axis=1, keepdims=True)
-    count_ref[...] = jnp.broadcast_to(total, count_ref.shape).astype(jnp.int32)
-    by_tile_ref[...] = ones_where(
-        (iota((own_tiles, cap), 0).astype(F32) == tiles) & (place_f < total)
-    )
+    held = (iota((own_tiles, cap), 0).astype(F32) == tiles) & (place_f < total)
+    by_tile = ones_where(held)
+    member = dot_t(by_row, by_tile)
+    rank = jnp.where(member > 0.5, dot_n(before, member.astype(BF16)), 384.0).astype(BF16)
+    place_high = jnp.floor(place_f * (1.0 / 32.0))
+    slot_high = dot_t(by_row * place_high.astype(BF16), by_tile).astype(BF16)
+    slot_low = dot_t(by_row * (place_f - 32.0 * place_high).astype(BF16), by_tile).astype(BF16)
+    held_count = jnp.sum(jnp.where(held, 1.0, 0.0), axis=1, keepdims=True)
+    group_count = jnp.floor((held_count + (GROUP - 1.0)) * (1.0 / GROUP))
+    earlier = ones_where(iota((own_tiles, own_tiles), 1) < iota((own_tiles, own_tiles), 0))
+    group_wide = jnp.broadcast_to(group_count, (own_tiles, TILE)).astype(BF16)
+    begin = dot_n(earlier, group_wide)[:, :1]
+    group = iota((own_tiles, groups), 1).astype(F32)
+    by_group_ref[...] = ones_where((begin <= group) & (group < begin + group_count))
+    spots = groups * GROUP
+    spot = iota((own_tiles, spots), 1).astype(F32) - GROUP * begin
+    inside = (spot >= 0.0) & (spot < held_count)
+    by_spot = ones_where(inside)
+    wanted = jnp.sum(jnp.where(inside, spot, 0.0), axis=0, keepdims=True)
+    filled = jnp.sum(jnp.where(inside, 1.0, 0.0), axis=0, keepdims=True)
+    match = (dot_n(rank, by_spot) == wanted) & (filled > 0.5)
+    slot = 32.0 * dot_n(slot_high, by_spot) + dot_n(slot_low, by_spot)
+    slots_ref[...] = jnp.sum(jnp.where(match, slot, 0.0), axis=0, keepdims=True).astype(jnp.int32)
+    row_of = iota((rows, spots), 0).astype(F32)
+    owner = jnp.sum(jnp.where(match, row_of, 0.0), axis=0, keepdims=True)
+    owners_ref[...] = jnp.where(filled > 0.5, owner, float(rows)).astype(jnp.int32)
+    all_groups = jnp.sum(group_count, axis=0, keepdims=True)
+    lane = iota(count_ref.shape, 1)
+    count_ref[...] = jnp.where(lane == 0, total, all_groups).astype(jnp.int32)
 
 
 def sum_slots(members, parts):
@@ -294,8 +320,8 @@
 
 def build_kernel(
     sup_hbm, src_hbm, tgt_hbm,
-    kern_ref, sum_ref, norm_ref, shift_ref, rows_out, tiles_out, count_out, by_row_ref, by_tile_ref,
-    left, extra, part, sup_ref, src_ref, tgt_ref, rows_ref, tiles_ref, count_ref, sems,
+    kern_ref, sum_ref, norm_ref, shift_ref, tiles_out, count_out, by_row_ref, slots_ref, owners_ref, by_group_ref,
+    left, minus, part, rows_out, sup_ref, src_ref, tgt_ref, rows_ref, tiles_ref, count_ref, sems,
 ):
     moves = [
         pltpu.make_async_copy(*pair, sems.at[i])
@@ -313,55 +339,73 @@
     for move in moves[:3]:
         move.start()
     moves[0].wait()
-    list_support(sup_ref, rows_out, tiles_out, count_out, by_row_ref, by_tile_ref)
+    list_support(sup_ref, tiles_out, count_out, rows_out, by_row_ref, slots_ref, owners_ref, by_group_ref)
     for move in moves[3:]:
         move.start()
     moves[1].wait()
     dim, tgt_count = tgt_ref.shape
-    row_count = extra.shape[0]
-    lane = iota((TILE, TILE), 1)
-
     def one_tgt(k, unused):
         block = tgt_ref[:, pl.ds(pl.multiple_of(k * TILE, TILE), TILE)].astype(F32)
-        wide = jnp.concatenate([block, jnp.zeros((TILE - dim, TILE), F32)], axis=0).T
-        half = -0.5 * jnp.sum(wide * wide, axis=1, keepdims=True)
-        a = half.astype(BF16).astype(F32)
-        b = (half - a).astype(BF16).astype(F32)
-        c = half - a - b
-        pieces = jnp.where(lane == dim, a, jnp.where(lane == dim + 1, b, jnp.where(lane == dim + 2, c, 1.0)))
-        left[k] = jnp.where(lane < dim, wide, jnp.where(lane < dim + 4, pieces, 0.0)).astype(BF16)
+        half = -0.5 * jnp.sum(block * block, axis=0, keepdims=True)
+        first = half.astype(BF16).astype(F32)
+        second = (half - first).astype(BF16).astype(F32)
+        third = half - first - second
+        line = iota((8, TILE), 0)
+        extra = jnp.where(line == 0, first, jnp.where(line == 1, second, jnp.where(line == 2, third, 1.0)))
+        extra = jnp.where(line < 4, extra, 0.0)
+        none = jnp.zeros((TILE - dim - 8, TILE), F32)
+        left[k] = jnp.concatenate([block, extra, none], axis=0).T.astype(BF16)
         return unused
 
-    lax.fori_loop(0, tgt_count // TILE, one_tgt, 0)
-    line = iota((16, TILE), 0)
+    lax.fori_loop(0, tgt_count // TILE, one_tgt, 0, unroll=8)
     moves[2].wait()
 
-    def one_src(r, unused):
-        block = src_ref[:, pl.ds(pl.multiple_of(r * TILE, TILE), TILE)].astype(F32)
-        norm = jnp.sum(block * block, axis=0, keepdims=True)
+    def eight_src(g, unused):
+        norms = []
+        for u in range(8):
+            at = pl.multiple_of((g * 8 + u) * TILE, TILE)
+            block = src_ref[:, pl.ds(at, TILE)].astype(F32)
+            norms.append(jnp.sum(block * block, axis=0, keepdims=True))
+        norm = jnp.concatenate(norms, axis=0)
+        at = pl.multiple_of(g * 8, 8)
+        norm_ref[pl.ds(at, 8), :] = norm
         part_shift = (jnp.sqrt(norm) * (SHIFT / (2.0 * SCALE))).astype(BF16).astype(F32)
-        norm_ref[pl.ds(r, 1), :] = norm
-        shift_ref[pl.ds(r, 1), :] = part_shift * (2.0 * SCALE)
-        extra[r] = jnp.where(line < 3, 1.0, jnp.where(line == 3, -part_shift, 0.0)).astype(BF16)
+        minus[pl.ds(at, 8), :] = -part_shift
+        shift_ref[pl.ds(at, 8), :] = part_shift * (2.0 * SCALE)
         return unused
 
-    lax.fori_loop(0, row_count, one_src, 0, unroll=8)
+    lax.fori_loop(0, norm_ref.shape[0] // 8, eight_src, 0, unroll=2)
     part[...] = jnp.zeros_like(part)
     for move in moves[3:]:
         move.wait()
+    line = iota((16, TILE), 0)
     pad = jnp.zeros((TILE - dim - 16, TILE), BF16)
+    none = jnp.zeros((TILE, TILE), BF16)
+
+    def right_of(q):
+        r = rows_ref[0, q]
+        block = src_ref[:, pl.ds(pl.multiple_of(r * TILE, TILE), TILE)]
+        extra = jnp.where(line < 3, 1.0, jnp.where(line == 3, minus[pl.ds(r, 1), :], 0.0)).astype(BF16)
+        return jnp.concatenate([block, extra, pad], axis=0)
 
     def step(g, unused):
         base = g * BUILD_UNROLL
-        for u in range(BUILD_UNROLL):
+        for u in range(0, BUILD_UNROLL, 2):
             q = base + u
-            r = rows_ref[0, q]
-            k = tiles_ref[0, q]
-            block = src_ref[:, pl.ds(pl.multiple_of(r * TILE, TILE), TILE)]
-            right = jnp.concatenate([block, extra[r], pad], axis=0)
-            entry = jnp.exp2(dot_n(left[k], right) * (2.0 * SCALE))
-            kern_ref[q] = entry.astype(BF16)
-            part[pl.ds(q, 1), :] = jnp.sum(entry, axis=0, keepdims=True)
+            lefts = jnp.concatenate([left[tiles_ref[0, q]], left[tiles_ref[0, q + 1]]], axis=1)
+            rights = jnp.concatenate(
+                [
+                    jnp.concatenate([right_of(q), none], axis=0),
+                    jnp.concatenate([none, right_of(q + 1)], axis=0),
+                ],
+                axis=1,
+            )
+            entry = jnp.exp2(dot_n(lefts, rights) * (2.0 * SCALE))
+            kern_ref[q] = entry[:, :TILE].astype(BF16)
+            kern_ref[q + 1] = entry[:, TILE:].astype(BF16)
+            sums = jnp.sum(entry, axis=0, keepdims=True)
+            part[pl.ds(q, 1), :] = sums[:, :TILE]
+            part[pl.ds(q + 1, 1), :] = sums[:, TILE:]
         return unused
 
     lax.fori_loop(0, pl.cdiv(count_ref[0, 0], BUILD_UNROLL), step, 0)
@@ -399,7 +443,7 @@
     kern_ref, count_ref, tiles_ref, log_hbm, total_ref, by_row_ref, out_ref, table, part, log_ref, sem
 ):
     total = total_ref[...]
-    start(log_hbm, log_ref, sem, total, table, part)
+    start(log_hbm, log_ref, sem, total, table.at[pl.ds(0, total.shape[0])], part)
 
     def step(g, unused):
         base = g * ROW_UNROLL
@@ -417,52 +461,55 @@
     out_ref[...] = poison(in_range(total, COL_LOW, COL_HIGH), out)
 
 
-def col_body(ok, kern_ref, count_ref, rows_ref, total, by_tile_ref, out_ref, table, part, log_hbm, log_ref, sem):
-    start(log_hbm, log_ref, sem, total, table, part)
-    none = jnp.zeros((16, TILE), BF16)
-
-    def step(g, unused):
-        base = g * COL_UNROLL
-        for u in range(0, COL_UNROLL, 4):
-            q = base + u
-            ab = two_rows(table, rows_ref[0, q], rows_ref[0, q + 1])
-            cd = two_rows(table, rows_ref[0, q + 2], rows_ref[0, q + 3])
-            weights = jnp.concatenate(
-                [jnp.concatenate([ab, none], axis=1), jnp.concatenate([none, cd], axis=1)], axis=0
-            )
-            four = jnp.concatenate(
-                [
-                    jnp.concatenate([kern_ref[q], kern_ref[q + 2]], axis=1),
-                    jnp.concatenate([kern_ref[q + 1], kern_ref[q + 3]], axis=1),
-                ],
-                axis=0,
-            )
-            got = dot_t(weights, four)
-            part[pl.ds(q, 1), :] = got[0:1, :TILE]
-            part[pl.ds(q + 1, 1), :] = got[8:9, TILE:]
-            part[pl.ds(q + 2, 1), :] = got[16:17, :TILE]
-            part[pl.ds(q + 3, 1), :] = got[24:25, TILE:]
+def col_body(ok, kern_ref, count_ref, slots_ref, owners_ref, total, by_group_ref, out_ref, table, part, log_hbm, log_ref, sem):
+    rows = total.shape[0]
+    table[pl.ds(rows, 8), :] = jnp.zeros((8, TILE), F32)
+    start(log_hbm, log_ref, sem, total, table.at[pl.ds(0, rows)], part)
+    ones = jnp.ones((16, TILE), BF16)
+
+    def weighed(spot):
+        weight = jnp.broadcast_to(table[pl.ds(owners_ref[0, spot], 1), :], (16, TILE)).astype(BF16)
+        return kern_ref[slots_ref[0, spot]] * jnp.concatenate([weight] * (TILE // 16), axis=0)
+
+    def group_sum(g):
+        terms = [weighed(g * GROUP + i) for i in range(GROUP)]
+        while len(terms) > 1:
+            terms = [a + b for a, b in zip(terms[::2], terms[1::2], strict=True)]
+        return terms[0]
+
+    def step(i, unused):
+        base = i * GROUP_UNROLL
+        for u in range(0, GROUP_UNROLL, 2):
+            g = base + u
+            got = dot_t(ones, jnp.concatenate([group_sum(g), group_sum(g + 1)], axis=0))
+            part[pl.ds(g, 1), :] = got[0:1, :TILE]
+            part[pl.ds(g + 1, 1), :] = got[0:1, TILE:]
         return unused
 
-    lax.fori_loop(0, pl.cdiv(count_ref[0, 0], COL_UNROLL), step, 0)
-    out_ref[...] = poison(ok, sum_slots(by_tile_ref[...], part[...]))
+    lax.fori_loop(0, pl.cdiv(count_ref[0, 1], GROUP_UNROLL), step, 0)
+    out_ref[...] = poison(ok, sum_slots(by_group_ref[...], part[...]))
 
 
 def first_col_kernel(
-    kern_ref, count_ref, rows_ref, log_hbm, total_ref, by_tile_ref, out_ref, table, part, log_ref, sem
+    kern_ref, count_ref, slots_ref, owners_ref, log_hbm, total_ref, by_group_ref, out_ref, table, part, log_ref, sem
 ):
     total = total_ref[...]
     ok = in_range(total, ROW_LOW, ROW_HIGH)
-    col_body(ok, kern_ref, count_ref, rows_ref, total, by_tile_ref, out_ref, table, part, log_hbm, log_ref, sem)
+    col_body(
+        ok, kern_ref, count_ref, slots_ref, owners_ref, total, by_group_ref, out_ref, table, part, log_hbm, log_ref, sem
+    )
 
 
 def next_col_kernel(
-    kern_ref, count_ref, rows_ref, log_hbm, total_ref, earlier_ref, by_tile_ref, out_ref, table, part, log_ref, sem
+    kern_ref, count_ref, slots_ref, owners_ref, log_hbm, total_ref, earlier_ref, by_group_ref, out_ref,
+    table, part, log_ref, sem,
 ):
     total = total_ref[...]
     ratio = total / earlier_ref[...]
     ok = in_range(total, ROW_LOW, ROW_HIGH) & in_range(ratio, 1.0 / RATIO, RATIO)
-    col_body(ok, kern_ref, count_ref, rows_ref, total, by_tile_ref, out_ref, table, part, log_hbm, log_ref, sem)
+    col_body(
+        ok, kern_ref, count_ref, slots_ref, owners_ref, total, by_group_ref, out_ref, table, part, log_hbm, log_ref, sem
+    )
 
 
 def ring_sum(value, axis, size, perm):
@@ -490,7 +537,8 @@
     log_rows = log_source.reshape(row_count, TILE)
     log_cols = log_target.reshape(tile_count, TILE)
     array = jax.ShapeDtypeStruct
-    kern, total, norm, shift, rows, tiles, count, by_row, by_tile = pl.pallas_call(
+    groups = -(-(cap // GROUP + tile_count) // GROUP_UNROLL) * GROUP_UNROLL
+    kern, total, norm, shift, tiles, count, by_row, slots, owners, by_group = pl.pallas_call(
         build_kernel,
         out_shape=(
             pltpu.VMEM((cap, TILE, TILE), BF16),
@@ -498,17 +546,19 @@
             array((row_count, TILE), F32),
             array((row_count, TILE), F32),
             array((1, cap), jnp.int32),
-            array((1, cap), jnp.int32),
             array((1, TILE), jnp.int32),
             array((row_count, cap), BF16),
-            array((tile_count, cap), BF16),
+            array((1, groups * GROUP), jnp.int32),
+            array((1, groups * GROUP), jnp.int32),
+            array((tile_count, groups), BF16),
         ),
         in_specs=[ANY] * 3,
-        out_specs=(VMEM,) * 9,
+        out_specs=(VMEM,) * 10,
         scratch_shapes=[
             pltpu.VMEM((tile_count, TILE, TILE), BF16),
-            pltpu.VMEM((row_count, 16, TILE), BF16),
+            pltpu.VMEM((row_count, TILE), F32),
             pltpu.VMEM((cap, TILE), F32),
+            pltpu.VMEM((1, cap), jnp.int32),
             pltpu.VMEM(support.shape[::-1], jnp.int32),
             pltpu.VMEM(source_cells.shape[::-1], BF16),
             pltpu.VMEM(target_cells.shape[::-1], BF16),
@@ -522,31 +572,31 @@
     )(support.T, source_cells.T, target_cells.T)
     kern = pltpu.with_memory_space_constraint(kern, pltpu.VMEM)
 
-    def call(body, name, slots, log, vmem, out_rows, table_rows):
+    def call(body, name, lists, log, vmem, out_rows, parts):
         return pl.pallas_call(
             body,
             out_shape=array((out_rows, TILE), F32),
-            in_specs=[VMEM, SMEM, SMEM, ANY] + [VMEM] * len(vmem),
+            in_specs=[VMEM] + [SMEM] * (1 + len(lists)) + [ANY] + [VMEM] * len(vmem),
             out_specs=VMEM,
             scratch_shapes=[
-                pltpu.VMEM((table_rows, TILE), F32),
-                pltpu.VMEM((cap, TILE), F32),
-                pltpu.VMEM((table_rows, TILE), F32),
+                pltpu.VMEM((log.shape[0] + 8, TILE), F32),
+                pltpu.VMEM((parts, TILE), F32),
+                pltpu.VMEM(log.shape, F32),
                 pltpu.SemaphoreType.DMA,
             ],
             compiler_params=params(20),
             name=name,
-        )(kern, count, slots, log, *vmem)
+        )(kern, count, *lists, log, *vmem)
+
+    def cols_of(body, name, totals):
+        return sum_over_src(
+            call(body, name, (slots, owners), log_rows, (*totals, by_group), tile_count, groups)
+        )
 
     first = sum_over_tgt(total)
-    cols = call(first_col_kernel, "first_col", rows, log_rows, (first, by_tile), tile_count, row_count)
-    cols = sum_over_src(cols)
-    second = call(row_kernel, "row", tiles, log_cols, (cols, by_row), row_count, tile_count)
-    second = sum_over_tgt(second)
-    cols = call(
-        next_col_kernel, "next_col", rows, log_rows, (second, first, by_tile), tile_count, row_count
-    )
-    cols = sum_over_src(cols)
+    cols = cols_of(first_col_kernel, "first_col", (first,))
+    second = sum_over_tgt(call(row_kernel, "row", (tiles,), log_cols, (cols, by_row), row_count, cap))
+    cols = cols_of(next_col_kernel, "next_col", (second, first))
     source_pot = norm + EPS * log_rows - EPS * (jnp.log(second) + LN2 * shift)
     target_pot = EPS * log_cols - EPS * jnp.log(cols)
     return lax.cond(

time: 1470 us -> 1450 us (0.986)
  Pallas kernels: 41 us -> 24.9 us
where the time goes in v3:
time: 1450 us
  other arithmetic  421 us (29%)
  matrix products  402 us (28%)
  waiting for transfers between devices  359 us (25%)
  blocking collectives  95.3 us (7%)
  local copies, waits for them, and re-layouts  81.4 us (6%)
  starting transfers between devices  40.9 us (3%)
  Pallas kernels  24.9 us (2%)
  between operations  14.5 us (1%)
    dot_general x64, matrix products, cost_tile(): jnp.einsum('bie,bje->bij', src_block, tgt_block, preferred_element_type=j...  349 us
    psum x2, waiting for transfers between devices, across_targets(): return (highest, lax.psum(totals * jnp.exp(maxima - highest), 'tgt'))  168 us
    pmax x2, waiting for transfers between devices, across_targets(): highest = lax.pmax(maxima, 'tgt')  165 us
    reduce_sum x32, other arithmetic, exp_of(): terms = jnp.sum(jnp.exp(scores - slot_max[:, :, None]), axis=2)  144 us
    reduce_sum x32, other arithmetic, exp_of(): terms = jnp.sum(jnp.exp(scores - slot_max[:, None, :]), axis=1)  144 us
    reduce_max x64, other arithmetic, fold_block(): jnp.max(jnp.where(selector[:, :, None] > 0.5, block_max[:, None, :], NEG)...  111 us
    pmax x2, blocking collectives, across_sources(): highest = lax.pmax(maxima, 'src')  48.2 us
    psum x2, blocking collectives, across_sources(): return (highest, lax.psum(totals * jnp.exp(maxima - highest), 'src'))  47.2 us
  transfers between devices with their start and end apart: 24, of which 17 were waited for; matrix products, arithmetic and copies ran while one was open for 0% of the time, Pallas kernels for 0%

profile of v3, /device:TPU:0, one launch (start us, length us, event | category | flops | bytes accessed | tf_op | source)
XLA Modules:
  0.0 1445.5 jit_solution(16203643362545659218)
XLA Ops:
  7.2 12.5 build.1
  31.1 6.1 collective-permute-start.3
  100.2 1338.8 %conditional.1 = (f32[32768]{0:T(1024)}, f32[8192]{0:T(1024)}) conditional(s32[]{:T(128)} %convert_element_type.59, (f32[32768]{0:T(1024)S(1)}, s32[256,32]{0,1:T(8,128)S(1)}, bf16[32768,64]{0,1:T(8,128)(2,1)}, bf16[8192,64]{0,1:T(8,128)(2,1)S(1)}, f32[8192]{0:T(1024)S(1)}) %tuple.188, (f32[256,128]{1,0:T(8,128)S(1)}, f32[256,128]{1,0:T(8,128)S(1)}, ...), branch_computations={%region_1.36_spmd, %region_36.37_spmd} | conditional | flops 801467648 | bytes 158626896 | solution.py:602
  101.3 5.6 copy_bitcast_fusion
  109.5 30.4 %scatter_custom_fusion = s32[1024]{0:T(1024)S(1)} fusion(s32[8192]{0:T(1024)S(1)} %bitcast.194, s32[8192]{0:T(1024)S(1)} %iota.59, s32[]{:T(128)} %constant.164.clone), kind=kCustom, calls=%fused_computation.224 | custom fusion | bytes 4100 | tf_op jit(solution)/shard_map/cond/branch_0_fun/scatter | solution.py:172
  140.0 6.2 gather_fusion
  146.3 13.5 gather_fusion.4
  162.6 15.7 %gather_fusion.3 = bf16[1024,128,64]{1,2,0:T(8,128)(2,1)} fusion(bf16[256,128,64]{1,2,0:T(8,128)(2,1)} %copy_bitcast_fusion, s32[1024]{0:T(1024)S(1)} %get-tuple-element.584), kind=kCustom, calls=%fused_computation.3 | custom fusion | bytes 33558528 | tf_op jit(solution)/shard_map/cond/branch_0_fun/gather | solution.py:179
  181.8 223.4 %while.48 = (s32[]{:T(128)}, f32[256,128]{1,0:T(8,128)S(1)}, f32[256,128]{1,0:T(8,128)S(1)}, s32[16,64]{1,0:T(8,128)S(1)}, pred[16,64]{1,0:T(8,128)(4,1)S(1)}, /...) while((s32[]{:T(128)}, f32[256,128]{1,0:T(8,128)S(1)}, ...), condition=%wide.region_12.12_spmd.clone, body=%wide.region_8.11_spmd.clone.sunk | while | flops 208982080 | bytes 12587404 | solution.py:98
  196.0 5.4 fusion.177
  210.0 5.4 fusion.177
  223.9 5.4 fusion.177
  237.9 5.4 fusion.177
  251.9 5.4 fusion.177
  265.8 5.4 fusion.177
  279.8 5.4 fusion.177
  293.7 5.4 fusion.177
  307.7 5.4 fusion.177
  321.7 5.4 fusion.177
  335.6 5.4 fusion.177
  349.6 5.4 fusion.177
  363.6 5.4 fusion.177
  377.5 5.4 fusion.177
  391.5 5.4 fusion.177
  405.9 85.6 %all-reduce.5.cloned.1.call-done = f32[256,128]{1,0:T(8,128)} async-done(((f32[256,128]{1,0:T(8,128)}), f32[256,128]{1,0:T(8,128)}) %all-reduce.5.cloned.1.call-update) | async-done | bytes 131088 | tf_op jit(solution)/shard_map/cond/branch_0_fun/pmax | solution.py:145
  493.5 83.8 %all-reduce.7.cloned.1.call-done = f32[256,128]{1,0:T(8,128)} async-done(((f32[256,128]{1,0:T(8,128)}), f32[256,128]{1,0:T(8,128)}) %all-reduce.7.cloned.1.call-update) | async-done | bytes 131088 | tf_op jit(solution)/shard_map/cond/branch_0_fun/psum | solution.py:146
  578.3 187.3 %while.49 = (s32[]{:T(128)}, f32[64,128]{1,0:T(8,128)S(1)}, f32[64,128]{1,0:T(8,128)S(1)}, s32[16,64]{1,0:T(8,128)S(1)}, pred[16,64]{1,0:T(8,128)(4,1)S(1)}, /*i...) while((s32[]{:T(128)}, f32[64,128]{1,0:T(8,128)S(1)}, ...), condition=%wide.region_19.19_spmd.clone, body=%wide.region_15.18_spmd.clone.sunk | while | flops 186740800 | bytes 11612564 | solution.py:141
  578.6 5.4 fusion.187
  602.0 5.4 fusion.187
  613.8 5.4 fusion.187
  625.5 5.4 fusion.187
  637.2 5.4 fusion.187
  660.6 5.4 fusion.187
  672.3 5.4 fusion.187
  684.0 5.4 fusion.187
  695.7 5.4 fusion.187
  707.4 5.4 fusion.187
  719.1 5.4 fusion.187
  730.8 5.4 fusion.187
  742.5 5.4 fusion.187
  754.3 5.4 fusion.187
  765.7 24.1 %pmax.25 = f32[64,128]{1,0:T(8,128)S(1)} all-reduce(f32[64,128]{1,0:T(8,128)S(1)} %get-tuple-element.267), channel_id=1, replica_groups=mesh['src'=8,'tgt'=16] {'src'}, use_global_device_ids=true, to_apply=%region_20.20 | all-reduce | flops 8192 | bytes 65536 | tf_op jit(solution)/shard_map/cond/branch_0_fun/pmax | solution.py:150
  789.8 23.6 %psum.25 = f32[64,128]{1,0:T(8,128)S(1)} all-reduce(f32[64,128]{1,0:T(8,128)S(1)} %exponential_multiply_fusion.3), channel_id=1, replica_groups=mesh['src'=8,'tgt'=16] {'src'}, use_global_device_ids=true, to_apply=%region_21.21 | all-reduce | flops 8192 | bytes 65536 | tf_op jit(solution)/shard_map/cond/branch_0_fun/psum | solution.py:151
  813.4 223.4 %while.50 = (s32[]{:T(128)}, f32[256,128]{1,0:T(8,128)S(1)}, f32[256,128]{1,0:T(8,128)S(1)}, s32[16,64]{1,0:T(8,128)S(1)}, pred[16,64]{1,0:T(8,128)(4,1)S(1)}, /...) while((s32[]{:T(128)}, f32[256,128]{1,0:T(8,128)S(1)}, ...), condition=%wide.region_26.26_spmd.clone, body=%wide.region_22.25_spmd.clone.sunk | while | flops 208982080 | bytes 12620180 | solution.py:98
  813.7 5.4 fusion.197
  827.6 5.4 fusion.197
  855.6 5.4 fusion.197
  869.5 5.4 fusion.197
  883.5 5.4 fusion.197
  1037.5 79.1 %all-reduce.9.cloned.1.call-done = f32[256,128]{1,0:T(8,128)} async-done(((f32[256,128]{1,0:T(8,128)}), f32[256,128]{1,0:T(8,128)}) %all-reduce.9.cloned.1.call-update) | async-done | bytes 131088 | tf_op jit(solution)/shard_map/cond/branch_0_fun/pmax | solution.py:145
  1118.4 84.0 %all-reduce.11.cloned.1.call-done = f32[256,128]{1,0:T(8,128)} async-done(((f32[256,128]{1,0:T(8,128)}), f32[256,128]{1,0:T(8,128)}) %all-reduce.11.cloned.1.call-update) | async-done | bytes 131088 | tf_op jit(solution)/shard_map/cond/branch_0_fun/psum | solution.py:146
  1203.3 187.3 %while.51 = (s32[]{:T(128)}, f32[64,128]{1,0:T(8,128)S(1)}, f32[64,128]{1,0:T(8,128)S(1)}, s32[16,64]{1,0:T(8,128)S(1)}, pred[16,64]{1,0:T(8,128)(4,1)S(1)}, /*i...) while((s32[]{:T(128)}, f32[64,128]{1,0:T(8,128)S(1)}, ...), condition=%wide.region_33.33_spmd.clone, body=%wide.region_29.32_spmd.clone.sunk | while | flops 186740800 | bytes 11612564 | solution.py:141
  1203.6 5.4 fusion.207
  1227.0 5.4 fusion.207
  1238.7 5.4 fusion.207
  1262.1 5.4 fusion.207
  1285.6 5.4 fusion.207
  1297.3 5.4 fusion.207
  1320.7 5.4 fusion.207
  1344.1 5.4 fusion.207
  1355.8 5.4 fusion.207
  1379.2 5.4 fusion.207
  1390.7 24.1 %pmax.27 = f32[64,128]{1,0:T(8,128)S(1)} all-reduce(f32[64,128]{1,0:T(8,128)S(1)} %get-tuple-element.271), channel_id=1, replica_groups=mesh['src'=8,'tgt'=16] {'src'}, use_global_device_ids=true, to_apply=%region_34.34 | all-reduce | flops 8192 | bytes 65536 | tf_op jit(solution)/shard_map/cond/branch_0_fun/pmax | solution.py:150
  1414.8 23.6 %psum.27 = f32[64,128]{1,0:T(8,128)S(1)} all-reduce(f32[64,128]{1,0:T(8,128)S(1)} %exponential_multiply_fusion.2), channel_id=1, replica_groups=mesh['src'=8,'tgt'=16] {'src'}, use_global_device_ids=true, to_apply=%region_35.35 | all-reduce | flops 8192 | bytes 65536 | tf_op jit(solution)/shard_map/cond/branch_0_fun/psum | solution.py:151
  (903 shorter events, 666.9 us)
Async XLA Ops:
  7.2 36.3 %copy-start.5 = (f32[32768]{0:T(1024)S(1)}, f32[32768]{0:T(1024)}, u32[]{:S(2)}) copy-start(f32[32768]{0:T(1024)} %param.17) | copy-start | bytes 393220
  19.7 6.6 collective-permute-start
  22.9 8.2 collective-permute-start.1
  23.5 7.6 collective-permute-start.2
  31.1 9.4 collective-permute-start.3
  37.3 6.2 collective-permute-start.4
  37.3 6.2 collective-permute-start.5
  43.5 14.3 copy-start.6
  47.8 1.3 collective-permute-start.6
  49.1 5.9 collective-permute-start.7
  51.7 5.1 collective-permute-start.8
  53.8 3.9 collective-permute-start.9
  61.7 7.7 collective-permute-start.10
  62.4 10.0 collective-permute-start.11
  65.2 7.2 collective-permute-start.12
  72.5 7.9 collective-permute-start.13
  75.0 7.3 collective-permute-start.14
  76.7 5.7 collective-permute-start.15
  82.4 17.8 %copy-start.3 = (bf16[8192,64]{0,1:T(8,128)(2,1)S(1)}, bf16[8192,64]{0,1:T(8,128)(2,1)}, u32[]{:S(2)}) copy-start(bf16[8192,64]{0,1:T(8,128)(2,1)} %param.16) | copy-start | bytes 3145732
  82.4 17.8 %copy-start.7 = (s32[256,32]{0,1:T(8,128)S(1)}, s32[256,32]{0,1:T(8,128)}, u32[]{:S(2)}) copy-start(s32[256,32]{0,1:T(8,128)} %param.19) | copy-start | bytes 98308
  86.7 2.8 collective-permute-start.16
  89.5 6.0 collective-permute-start.17
  92.3 5.1 collective-permute-start.18
  95.0 3.9 collective-permute-start.19
  100.2 391.4 %all-reduce.5.cloned.1.call-start = ((), (), s32[]{:S(2)}) async-start(), calls=%async_computation | async-start | bytes 262144 | tf_op jit(solution)/shard_map/cond/branch_0_fun/pmax | solution.py:145
  101.2 5.6 copy-start
  405.2 0.7 copy-start.2
  405.9 171.5 %all-reduce.7.cloned.1.call-start = ((), (), s32[]{:S(2)}) async-start(), calls=%async_computation.1 | async-start | bytes 262144 | tf_op jit(solution)/shard_map/cond/branch_0_fun/psum | solution.py:146
  493.2 623.4 %all-reduce.9.cloned.1.call-start = ((), (), s32[]{:S(2)}) async-start(), calls=%async_computation.2 | async-start | bytes 262144 | tf_op jit(solution)/shard_map/cond/branch_0_fun/pmax | solution.py:145
  1036.8 0.7 copy-start.1
  1037.5 164.8 %all-reduce.11.cloned.1.call-start = ((), (), s32[]{:S(2)}) async-start(), calls=%async_computation.3 | async-start | bytes 262144 | tf_op jit(solution)/shard_map/cond/branch_0_fun/psum | solution.py:146
  1390.7 48.3 %copy-start.4 = (f32[256,128]{1,0:T(8,128)}, f32[256,128]{1,0:T(8,128)S(1)}, u32[]{:S(2)}) copy-start(f32[256,128]{1,0:T(8,128)S(1)} %get-tuple-element.1092) | copy-start | bytes 393220 | tf_op jit(solution)/shard_map/cond
Sparse Core Ops, SparseCore 0:
  406.0 85.5 all-reduce.4
  495.7 81.6 all-reduce.6
  1037.6 79.0 all-reduce.8
  1120.6 81.6 all-reduce.10
